TPU v7x, 128 devices: a whole 4x4x4 slice. The times are simulated.
128 devices in a mesh: rep: 16 (over z, y_lo, core), shard: 8 (over x, y_hi).
Axes of the slice: x: 4, y: 4 (y_hi: 2, y_lo: 2; y = y_hi * 2 + y_lo), z: 4, core: 2. Of those that a mesh axis runs over, the one named last changes fastest.
Arguments:
- tokens: bfloat16 [16384, 2048], P(('rep', 'shard')), may hold values from -6 to 6
- lengths: int32 [16], P('rep'), may hold values from 256 to 1024, as said below
- vectors: float32 [8, 2048], P(None, 'shard'), may hold values from -0.9 to 1.75
- fc1_bias: float32 [8192], P('shard'), may hold values from -1.8 to 1.8
- w_qkv: bfloat16 [2048, 6144], P('shard'), may hold values from -0.125 to 0.125
- w_dense: bfloat16 [2048, 2048], P('shard'), may hold values from -0.5 to 0.5
- w_fc1: bfloat16 [2048, 8192], P('shard'), may hold values from -0.125 to 0.125
- w_fc2: bfloat16 [8192, 2048], P('shard'), may hold values from -0.0625 to 0.0625
- cotangent: bfloat16 [16384, 2048], P(('rep', 'shard')), may hold values from -12 to 12
Outputs:
- output: bfloat16 [16384, 2048], P(('rep', 'shard'))
- d_tokens: bfloat16 [16384, 2048], P(('rep', 'shard'))
- g_vectors: float32 [8, 2048], P(None, 'shard')
- g_fc1_bias: float32 [8192], P('shard')
- g_w_qkv: float32 [2048, 6144], P('shard')
- g_w_dense: float32 [2048, 2048], P('shard')
- g_w_fc1: float32 [2048, 8192], P('shard')
- g_w_fc2: float32 [8192, 2048], P('shard')
Inputs may be any that keep to these rules, and one draw needn't show every extreme that they name: `lengths`: some slot has length exactly 1024 and another exactly 256.
All inputs are finite; a program needn't handle non-finite values.
Results may differ from a plain program's by a relative error of at most 0.025.
Values may be sent and summed in bfloat16 or wider, within the bound.
No kernel may reach another device: no remote copies, remote signals or barrier semaphores. Data moves between devices by JAX's collectives and lax.ppermute only.
A program may use at most 384 MiB of HBM per device.

v0:
```python
import jax
import jax.numpy as jnp
from jax import lax
from jax.sharding import PartitionSpec as P

HEAD_DIM = 64


epsilon = 1e-05


def layer_norm(values, gain_row, shift_row):
    average = jnp.mean(values, axis=-1, keepdims=True)
    centred = values - average
    variance = jnp.mean(centred * centred, axis=-1, keepdims=True)
    inverse = lax.rsqrt(variance + epsilon)
    normed = centred * inverse
    return (normed * gain_row + shift_row, normed, inverse)


def norm_back(grad_out, normed, inverse, gain_row):
    scaled = grad_out * gain_row
    inner = (
        scaled
        - jnp.mean(scaled, axis=-1, keepdims=True)
        - normed * jnp.mean(scaled * normed, axis=-1, keepdims=True)
    )
    return (inner * inverse, jnp.sum(grad_out * normed, 0), jnp.sum(grad_out, 0))


def project(acts, weight):
    return (
        jnp.dot(
            acts,
            lax.all_gather(weight, "shard", axis=0, tiled=True),
            preferred_element_type=jnp.float32,
        ),
        weight,
    )


def project_back(grad_b, kept):
    contract = (((1,), (1,)), ((), ()))
    return lax.dot_general(
        grad_b,
        lax.all_gather(kept, "shard", axis=0, tiled=True),
        contract,
        preferred_element_type=jnp.float32,
    )


def weight_grad(acts_b, grad_b):
    tokens_first = (((0,), (0,)), ((), ()))
    return lax.psum_scatter(
        lax.dot_general(acts_b, grad_b, tokens_first, preferred_element_type=jnp.float32).astype(
            jnp.bfloat16
        ),
        "shard",
        scatter_dimension=0,
        tiled=True,
    ).astype(jnp.float32)


def column_sums(values):
    return jnp.sum(values.astype(jnp.float32), 0)


def local(tokens, lengths, vectors, fc1_bias, w_qkv, w_dense, w_fc1, w_fc2, cotangent):
    width = tokens.shape[1]
    dev_rows = tokens.shape[0]
    shard_count = lax.axis_size("shard")
    shard_pos = lax.axis_index("shard")
    slot_rows = dev_rows * shard_count
    head_count = width // HEAD_DIM
    scale = HEAD_DIM ** (-0.5)
    bf16 = jnp.bfloat16
    f32 = jnp.float32
    all_vectors, all_fc1_bias = (
        lax.all_gather(vectors, "shard", axis=1, tiled=True),
        lax.all_gather(fc1_bias, "shard", axis=0, tiled=True),
    )
    query_pos = jnp.arange(dev_rows, dtype=jnp.int32) * shard_count + shard_pos
    key_index = jnp.arange(slot_rows, dtype=jnp.int32)
    key_pos = key_index % dev_rows * shard_count + key_index // dev_rows
    valid_rows = (query_pos < lengths[0]).astype(f32)[:, None]
    slopes = jnp.exp2(-8.0 * (jnp.arange(head_count, dtype=f32) + 1.0) / head_count)
    distance = (key_pos[None, :] - query_pos[:, None]).astype(f32)
    alibi_bias = slopes[:, None, None] * distance[None]
    causal = (key_pos[None, :] <= query_pos[:, None])[None]

    def scores_of(query_heads, key_heads):
        raw = jnp.einsum("qhd,khd->hqk", query_heads, key_heads, preferred_element_type=f32)
        return jnp.where(causal, raw * scale + alibi_bias, -1e30)

    inputs = tokens.astype(f32)
    normed_one, unit_one, inverse_one = layer_norm(inputs, all_vectors[0], all_vectors[1])
    normed_one_b = normed_one.astype(bf16)
    projected, kept_qkv = project(normed_one_b, w_qkv)
    query_b = (projected[:, :width] + all_vectors[2]).astype(bf16)
    key_b = projected[:, width : 2 * width].astype(bf16)
    value_b = (projected[:, 2 * width :] + all_vectors[3]).astype(bf16)
    key_all, value_all = (
        lax.all_gather(key_b, "shard", axis=0, tiled=True),
        lax.all_gather(value_b, "shard", axis=0, tiled=True),
    )
    query_heads = query_b.reshape(dev_rows, head_count, HEAD_DIM)
    key_heads = key_all.reshape(slot_rows, head_count, HEAD_DIM)
    value_heads = value_all.reshape(slot_rows, head_count, HEAD_DIM)
    scores = scores_of(query_heads, key_heads)
    row_max = jnp.max(scores, axis=-1, keepdims=True)
    exponent = jnp.exp(scores - row_max)
    row_total = jnp.sum(exponent, axis=-1, keepdims=True)
    log_total = row_max + jnp.log(row_total)
    attention_b = (exponent / row_total).astype(bf16)
    context = jnp.einsum("hqk,khd->qhd", attention_b, value_heads, preferred_element_type=f32)
    context_b = context.reshape(dev_rows, width).astype(bf16)
    dense_out, kept_dense = project(context_b, w_dense)
    hidden = inputs + dense_out + all_vectors[4]
    normed_two, unit_two, inverse_two = layer_norm(hidden, all_vectors[5], all_vectors[6])
    normed_two_b = normed_two.astype(bf16)
    fc1_out, kept_fc1 = project(normed_two_b, w_fc1)
    pre_act = fc1_out + all_fc1_bias
    activated, gelu_back = jax.vjp(lambda values: jax.nn.gelu(values, approximate=False), pre_act)
    activated_b = activated.astype(bf16)
    fc2_out, kept_fc2 = project(activated_b, w_fc2)
    output = (valid_rows * (hidden + fc2_out + all_vectors[7])).astype(bf16)
    grad_mlp = valid_rows * cotangent.astype(f32)
    grad_mlp_b = grad_mlp.astype(bf16)
    grad_fc2 = weight_grad(activated_b, grad_mlp_b)
    grad_act_b = project_back(grad_mlp_b, kept_fc2).astype(bf16)
    grad_pre_b = gelu_back(grad_act_b.astype(f32))[0].astype(bf16)
    grad_fc1 = weight_grad(normed_two_b, grad_pre_b)
    grad_normed_two = project_back(grad_pre_b, kept_fc1)
    back_two, gain_two, shift_two = norm_back(
        grad_normed_two, unit_two, inverse_two, all_vectors[5]
    )
    grad_hidden = grad_mlp + back_two
    grad_hidden_b = grad_hidden.astype(bf16)
    grad_dense = weight_grad(context_b, grad_hidden_b)
    grad_ctx_b = project_back(grad_hidden_b, kept_dense).astype(bf16)
    grad_ctx_heads = grad_ctx_b.reshape(dev_rows, head_count, HEAD_DIM)
    attention = jnp.exp(scores_of(query_heads, key_heads) - log_total)
    again_b = attention.astype(bf16)
    grad_prob = jnp.einsum("qhd,khd->hqk", grad_ctx_heads, value_heads, preferred_element_type=f32)
    row_inner = jnp.sum(attention * grad_prob, axis=-1, keepdims=True)
    grad_score_b = (attention * (grad_prob - row_inner)).astype(bf16)
    grad_query_b = (
        (jnp.einsum("hqk,khd->qhd", grad_score_b, key_heads, preferred_element_type=f32) * scale)
        .reshape(dev_rows, width)
        .astype(bf16)
    )
    grad_key_part = (
        jnp.einsum("hqk,qhd->khd", grad_score_b, query_heads, preferred_element_type=f32) * scale
    ).reshape(slot_rows, width)
    grad_value_part = jnp.einsum(
        "hqk,qhd->khd", again_b, grad_ctx_heads, preferred_element_type=f32
    ).reshape(slot_rows, width)
    grad_key_own, grad_value_own = (
        lax.psum_scatter(
            grad_key_part.astype(jnp.bfloat16), "shard", scatter_dimension=0, tiled=True
        ).astype(jnp.float32),
        lax.psum_scatter(
            grad_value_part.astype(jnp.bfloat16), "shard", scatter_dimension=0, tiled=True
        ).astype(jnp.float32),
    )
    grad_key_b = grad_key_own.astype(bf16)
    grad_value_b = grad_value_own.astype(bf16)
    grad_proj_b = jnp.concatenate([grad_query_b, grad_key_b, grad_value_b], 1)
    grad_qkv = weight_grad(normed_one_b, grad_proj_b)
    grad_normed_one = project_back(grad_proj_b, kept_qkv)
    back_one, gain_one, shift_one = norm_back(
        grad_normed_one, unit_one, inverse_one, all_vectors[0]
    )
    d_tokens = (grad_hidden + back_one).astype(bf16)
    vector_terms = jnp.stack(
        [
            gain_one,
            shift_one,
            column_sums(grad_query_b),
            column_sums(grad_value_b),
            column_sums(grad_hidden_b),
            gain_two,
            shift_two,
            jnp.sum(grad_mlp, 0),
        ]
    )
    bias_terms = column_sums(grad_pre_b)
    vector_share, bias_share = (
        lax.psum_scatter(
            vector_terms.astype(jnp.bfloat16), "shard", scatter_dimension=1, tiled=True
        ).astype(jnp.float32),
        lax.psum_scatter(
            bias_terms.astype(jnp.bfloat16), "shard", scatter_dimension=0, tiled=True
        ).astype(jnp.float32),
    )
    summed = (
        lax.psum(vector_share.astype(jnp.bfloat16), "rep").astype(jnp.float32),
        lax.psum(bias_share.astype(jnp.bfloat16), "rep").astype(jnp.float32),
        lax.psum(grad_qkv.astype(jnp.bfloat16), "rep").astype(jnp.float32),
        lax.psum(grad_dense.astype(jnp.bfloat16), "rep").astype(jnp.float32),
        lax.psum(grad_fc1.astype(jnp.bfloat16), "rep").astype(jnp.float32),
        lax.psum(grad_fc2.astype(jnp.bfloat16), "rep").astype(jnp.float32),
    )
    return (output, d_tokens, summed[0], summed[1], summed[2], summed[3], summed[4], summed[5])


def solution(mesh):
    return jax.shard_map(
        local,
        mesh=mesh,
        in_specs=(
            P(("rep", "shard"), None),
            P("rep"),
            P(None, "shard"),
            P("shard"),
            P("shard", None),
            P("shard", None),
            P("shard", None),
            P("shard", None),
            P(("rep", "shard"), None),
        ),
        out_specs=(
            P(("rep", "shard"), None),
            P(("rep", "shard"), None),
            P(None, "shard"),
            P("shard"),
            P("shard", None),
            P("shard", None),
            P("shard", None),
            P("shard", None),
        ),
        check_vma=False,
    )
```

profile of v0, /device:TPU:63, one launch (start us, length us, event | category | flops | bytes accessed | tf_op | source)
XLA Modules:
  0.0 2936.6 jit_solution(6187366406651012423)
XLA Ops:
  8.0 28.1 all_gather.28
  39.3 232.4 %all-gather.7.cloned.1.call-done = bf16[2048,6144]{1,0:T(8,128)(2,1)} async-done(((bf16[256,6144]{1,0:T(8,128)(2,1)}), bf16[2048,6144]{1,0:T(8,128)(2,1)}) %all-gather.7.cloned.1.call-update) | async-done | bytes 25165840 | tf_op jit(solution)/shard_map/all_gather | solution.py:35
  289.2 28.0 all_gather.34
  317.7 36.6 %all-gather.9.cloned.1.call-done = bf16[1024,2048]{1,0:T(8,128)(2,1)} async-done(((bf16[128,2048]{1,0:T(8,128)(2,1)}), bf16[1024,2048]{1,0:T(8,128)(2,1)}) %all-gather.9.cloned.1.call-update) | async-done | bytes 4194320 | tf_op jit(solution)/shard_map/all_gather | solution.py:104
  360.7 66.0 %all-gather.11.cloned.1.call-done = bf16[1024,2048]{1,0:T(8,128)(2,1)} async-done(((bf16[128,2048]{1,0:T(8,128)(2,1)}), bf16[1024,2048]{1,0:T(8,128)(2,1)}) %all-gather.11.cloned.1.call-update) | async-done | bytes 4194320 | tf_op jit(solution)/shard_map/all_gather | solution.py:103
  451.5 84.2 %all-gather.13.cloned.1.call-done = bf16[2048,2048]{1,0:T(8,128)(2,1)} async-done(((bf16[256,2048]{1,0:T(8,128)(2,1)}), bf16[2048,2048]{1,0:T(8,128)(2,1)}) %all-gather.13.cloned.1.call-update) | async-done | bytes 8388624 | tf_op jit(solution)/shard_map/all_gather | solution.py:35
  540.7 335.1 %all-gather.15.cloned.1.call-done = bf16[2048,8192]{1,0:T(8,128)(2,1)} async-done(((bf16[256,8192]{1,0:T(8,128)(2,1)}), bf16[2048,8192]{1,0:T(8,128)(2,1)}) %all-gather.15.cloned.1.call-update) | async-done | bytes 33554448 | tf_op jit(solution)/shard_map/all_gather | solution.py:35
  875.8 17.7 convolution_add_fusion
  893.5 322.4 %all-gather.17.cloned.1.call-done = bf16[8192,2048]{1,0:T(8,128)(2,1)} async-done(((bf16[1024,2048]{1,0:T(8,128)(2,1)}), bf16[8192,2048]{1,0:T(8,128)(2,1)}) %all-gather.17.cloned.1.call-update) | async-done | bytes 33554448 | tf_op jit(solution)/shard_map/all_gather | solution.py:35
  1216.0 26.7 fusion.64
  1242.6 19.5 multiply_reduce_fusion.1
  1290.8 16.8 multiply_reduce_fusion
  1345.3 28.3 reduce-scatter.24.cloned.1.call-done
  1375.6 85.5 %reduce-scatter.22.cloned.1.call-done = bf16[128,2048]{1,0:T(8,128)(2,1)} async-done(((bf16[1024,2048]{1,0:T(8,128)(2,1)}), bf16[128,2048]{1,0:T(8,128)(2,1)}) %reduce-scatter.22.cloned.1.call-update) | async-done | bytes 524304
  1476.5 23.5 convolution_convert_fusion.1
  1500.7 15.7 convolution_convert_fusion
  1534.2 45.2 %reduce-scatter.16.cloned.1.call-done = bf16[256,2048]{1,0:T(8,128)(2,1)} async-done(((bf16[2048,2048]{1,0:T(8,128)(2,1)}), bf16[256,2048]{1,0:T(8,128)(2,1)}) %reduce-scatter.16.cloned.1.call-update) | async-done | bytes 1048592 | tf_op jit(solution)/shard_map/reduce_scatter | solution.py:54
  1579.4 265.5 %reduce-scatter.14.cloned.1.call-done = bf16[256,6144]{1,0:T(8,128)(2,1)} async-done(((bf16[2048,6144]{1,0:T(8,128)(2,1)}), bf16[256,6144]{1,0:T(8,128)(2,1)}) %reduce-scatter.14.cloned.1.call-update) | async-done | bytes 3145744 | tf_op jit(solution)/shard_map/reduce_scatter | solution.py:54
  1844.8 357.4 %reduce-scatter.20.cloned.1.call-done = bf16[1024,2048]{1,0:T(8,128)(2,1)} async-done(((bf16[8192,2048]{1,0:T(8,128)(2,1)}), bf16[1024,2048]{1,0:T(8,128)(2,1)}) %reduce-scatter.20.cloned.1.call-update) | async-done | bytes 4194320 | tf_op jit(solution)/shard_map/reduce_scatter | solution.py:54
  2202.3 358.7 %reduce-scatter.18.cloned.1.call-done = bf16[256,8192]{1,0:T(8,128)(2,1)} async-done(((bf16[2048,8192]{1,0:T(8,128)(2,1)}), bf16[256,8192]{1,0:T(8,128)(2,1)}) %reduce-scatter.18.cloned.1.call-update) | async-done | bytes 4194320 | tf_op jit(solution)/shard_map/reduce_scatter | solution.py:54
  2562.9 29.8 %all-reduce = bf16[8192]{0:T(1024)(128)(2,1)S(1)} all-reduce(bf16[8192]{0:T(1024)(128)(2,1)S(1)} %copy-done.22), channel_id=5, replica_groups=mesh['rep'=16,'shard'=8] {'shard'}, use_global_device_ids=true, to_apply=%region_24.25.clone | all-reduce | flops 8192 | bytes 32768
  2592.7 20.5 fusion.19
  2628.2 23.8 all-reduce.1
  2653.2 261.4 %all-reduce.5.cloned.1.call-done = (bf16[256,6144]{1,0:T(8,128)(2,1)}, bf16[256,2048]{1,0:T(8,128)(2,1)}, bf16[256,8192]{1,0:T(8,128)(2,1)}, bf16[1024,2048]{1,0:T(8,128)(2,1)}) async-done(((bf16[256,6144]{1,0:T(8,128)(2,1)}, bf16[256,2048]{1,0:T(8,128)(2,1)}, bf16[256,8192]{1,0:T(8,128)(2,1)}, bf16[1024,2048]{1,0:T(8,128)(2,1)}), (bf16[256,6144]{1,0:T(8,128)(2,1)}, bf16[256,2048]{1,0:T(8,128)(2,1)}, ...) | async-done | bytes 12582928 | tf_op jit(solution)/shard_map/psum | solution.py:199
  (143 shorter events, 192.0 us)
Async XLA Ops:
  7.2 264.5 %copy-start.2 = (bf16[128,2048]{1,0:T(8,128)(2,1)S(1)}, bf16[128,2048]{1,0:T(8,128)(2,1)}, u32[]{:S(2)}) copy-start(bf16[128,2048]{1,0:T(8,128)(2,1)} %param.9) | copy-start | bytes 1572868
  7.2 264.5 %all-gather.7.cloned.1.call-start = ((), (), s32[]{:S(2)}) async-start(), calls=%async_computation.7 | async-start | bytes 28311552 | tf_op jit(solution)/shard_map/all_gather | solution.py:35
  7.9 346.4 %all-gather.9.cloned.1.call-start = ((), (), s32[]{:S(2)}) async-start(), calls=%async_computation.8 | async-start | bytes 4718592 | tf_op jit(solution)/shard_map/all_gather | solution.py:104
  37.3 244.5 %copy-start.18 = (f32[128]{0:T(128)}, f32[128]{0:T(128)S(1)}, u32[]{:S(2)}) copy-start(f32[128]{0:T(128)S(1)} %broadcast_multiply_fusion.5) | copy-start | bytes 1540
  38.6 243.2 %copy-start.20 = (f32[128]{0:T(128)}, f32[128]{0:T(128)S(1)}, u32[]{:S(2)}) copy-start(f32[128]{0:T(128)S(1)} %add_rsqrt_fusion.1) | copy-start | bytes 1540
  39.3 242.5 %copy-start.12 = (f32[1,2048]{1,0:T(1,128)}, f32[1,2048]{1,0:T(1,128)S(1)}, u32[]{:S(2)}) copy-start(f32[1,2048]{1,0:T(1,128)S(1)} %get-tuple-element.33) | copy-start | bytes 24580
  39.3 242.6 %copy-start.14 = (f32[1,2048]{1,0:T(1,128)}, f32[1,2048]{1,0:T(1,128)S(1)}, u32[]{:S(2)}) copy-start(f32[1,2048]{1,0:T(1,128)S(1)} %get-tuple-element.32) | copy-start | bytes 24580
  39.3 836.5 %copy-start.16 = (f32[1,2048]{1,0:T(1,128)}, f32[1,2048]{1,0:T(1,128)S(1)}, u32[]{:S(2)}) copy-start(f32[1,2048]{1,0:T(1,128)S(1)} %get-tuple-element.28) | copy-start | bytes 24580
  284.5 142.2 %all-gather.11.cloned.1.call-start = ((), (), s32[]{:S(2)}) async-start(), calls=%async_computation.9 | async-start | bytes 4718592 | tf_op jit(solution)/shard_map/all_gather | solution.py:103
  286.7 249.0 %all-gather.13.cloned.1.call-start = ((), (), s32[]{:S(2)}) async-start(), calls=%async_computation.10 | async-start | bytes 9437184 | tf_op jit(solution)/shard_map/all_gather | solution.py:35
  287.3 588.5 %all-gather.15.cloned.1.call-start = ((), (), s32[]{:S(2)}) async-start(), calls=%async_computation.11 | async-start | bytes 37748736 | tf_op jit(solution)/shard_map/all_gather | solution.py:35
  287.9 928.1 %all-gather.17.cloned.1.call-start = ((), (), s32[]{:S(2)}) async-start(), calls=%async_computation.12 | async-start | bytes 37748736 | tf_op jit(solution)/shard_map/all_gather | solution.py:35
  288.4 1085.1 %reduce-scatter.24.cloned.1.call-start = ((), (), s32[]{:S(2)}) async-start(), calls=%async_computation.19 | async-start | bytes 4718592
  875.8 340.2 %copy-start.10 = (bf16[128,2048]{1,0:T(8,128)(2,1)S(1)}, bf16[128,2048]{1,0:T(8,128)(2,1)}, u32[]{:S(2)}) copy-start(bf16[128,2048]{1,0:T(8,128)(2,1)} %param.17) | copy-start | bytes 1572868
  1290.7 170.3 %reduce-scatter.22.cloned.1.call-start = ((), (), s32[]{:S(2)}) async-start(), calls=%async_computation.18 | async-start | bytes 4718592
  1331.4 247.9 %reduce-scatter.16.cloned.1.call-start = ((), (), s32[]{:S(2)}) async-start(), calls=%async_computation.15 | async-start | bytes 9437184 | tf_op jit(solution)/shard_map/reduce_scatter | solution.py:54
  1337.4 125.7 %copy-start.13 = (f32[1,2048]{1,0:T(1,128)S(1)}, f32[1,2048]{1,0:T(1,128)}, u32[]{:S(2)}) copy-start(f32[1,2048]{1,0:T(1,128)} %copy-done.12) | copy-start | bytes 24580
  1337.4 125.7 %copy-start.15 = (f32[1,2048]{1,0:T(1,128)S(1)}, f32[1,2048]{1,0:T(1,128)}, u32[]{:S(2)}) copy-start(f32[1,2048]{1,0:T(1,128)} %copy-done.14) | copy-start | bytes 24580
  1337.4 125.7 %copy-start.19 = (f32[128]{0:T(128)S(1)}, f32[128]{0:T(128)}, u32[]{:S(2)}) copy-start(f32[128]{0:T(128)} %copy-done.18) | copy-start | bytes 1540
  1337.5 507.4 %reduce-scatter.14.cloned.1.call-start = ((), (), s32[]{:S(2)}) async-start(), calls=%async_computation.14 | async-start | bytes 28311552 | tf_op jit(solution)/shard_map/reduce_scatter | solution.py:54
  1476.2 726.0 %reduce-scatter.20.cloned.1.call-start = ((), (), s32[]{:S(2)}) async-start(), calls=%async_computation.17 | async-start | bytes 37748736 | tf_op jit(solution)/shard_map/reduce_scatter | solution.py:54
  1500.0 1061.0 %reduce-scatter.18.cloned.1.call-start = ((), (), s32[]{:S(2)}) async-start(), calls=%async_computation.16 | async-start | bytes 37748736 | tf_op jit(solution)/shard_map/reduce_scatter | solution.py:54
  1516.4 1111.8 %reduce-scatter.12.cloned.1.call-start = ((), (), s32[]{:S(2)}) async-start(), calls=%async_computation.13 | async-start | bytes 36864 | tf_op jit(solution)/shard_map/reduce_scatter | solution.py:189
  1534.2 1380.5 %all-reduce.5.cloned.1.call-start = ((), (), s32[]{:S(2)}) async-start(), calls=%async_computation.20 | async-start | bytes 25165824 | tf_op jit(solution)/shard_map/psum | solution.py:199
  (16 other events, 342.6 us)
Sparse Core Ops, SparseCore 0:
  10.4 261.2 all-gather.6
  284.6 69.5 all-gather.8
  357.2 69.4 all-gather.10
  428.9 106.7 all-gather.12
  537.9 337.9 all-gather.14
  878.0 337.9 all-gather.16
  1290.9 82.6 reduce-scatter.23
  1377.4 83.6 reduce-scatter.21
  1465.5 113.8 reduce-scatter.15
  1583.2 261.6 reduce-scatter.13
  1849.3 352.8 reduce-scatter.19
  2206.6 354.3 reduce-scatter.17
  2565.3 62.8 reduce-scatter.11
  2630.9 283.7 all-reduce.4
where the time goes:
time: 2940 us
  waiting for transfers between devices  2490 us (85%)
  matrix products  229 us (8%)
  blocking collectives  110 us (4%)
  local copies, waits for them, and re-layouts  43.8 us (1%)
  other arithmetic  42.4 us (1%)
    reduce_scatter x4, waiting for transfers between devices, weight_grad(): lax.psum_scatter(lax.dot_general(acts_b, grad_b, tokens_first, preferred_...  1030 us
    all_gather x4, waiting for transfers between devices, project(): lax.all_gather(weight, 'shard', axis=0, tiled=True)  974 us
    psum x1, waiting for transfers between devices, local(): lax.psum(grad_qkv.astype(jnp.bfloat16), 'rep').astype(jnp.float32)  261 us
    unnamed x16, waiting for transfers between devices  116 us
    dot_general x4, matrix products, project_back(): lax.dot_general(grad_b, lax.all_gather(kept, 'shard', axis=0, tiled=True)...  67.6 us
    all_gather x1, waiting for transfers between devices, local(): lax.all_gather(key_b, 'shard', axis=0, tiled=True)  66 us
  transfers between devices with their start and end apart: 14, of which 14 were waited for; matrix products, arithmetic and copies ran while one was open for 7% of the time, Pallas kernels for 0%

commit v1 on v0

v1 whole, which is shorter than its diff:
```python
import numpy as np
import jax
import jax.numpy as jnp
from jax import lax
from jax.sharding import Mesh
from jax.sharding import PartitionSpec as P

HEAD_DIM = 64
EPSILON = 1e-05
bf16 = jnp.bfloat16
f32 = jnp.float32

ALL = ("z", "yl", "c", "x", "yh")
NX, NZ = 4, 4
SWAP = [(0, 0), (1, 2), (2, 1), (3, 3)]


def move(values):
    return lax.ppermute(values, ("c", "yh"), SWAP)


def across_core(values):
    return lax.ppermute(values, "c", [(0, 1), (1, 0)])


def along_x(values, step):
    return lax.ppermute(values, "x", [(i, (i + step) % NX) for i in range(NX)])


def along_z(values, step):
    return lax.ppermute(values, "z", [(i, (i + step) % NZ) for i in range(NZ)])


def gather_rows(block):
    other = across_core(block)
    mine = [along_x(block, k) for k in (1, 3, 2)]
    theirs = across_core(jnp.stack(mine))
    return jnp.stack(
        [
            jnp.stack([block, other]),
            jnp.stack([mine[0], theirs[0]]),
            jnp.stack([mine[2], theirs[2]]),
            jnp.stack([mine[1], theirs[1]]),
        ]
    )


def scatter_rows(parts):
    sent = across_core(parts[:, 1].astype(bf16))
    chip = parts[:, 0] + sent.astype(f32)
    got = [along_x(chip[k].astype(bf16), -k) for k in (2, 1, 3)]
    return chip[0] + got[0].astype(f32) + got[1].astype(f32) + got[2].astype(f32)


def normalize(values):
    average = jnp.mean(values, axis=-1, keepdims=True)
    centred = values - average
    variance = jnp.mean(centred * centred, axis=-1, keepdims=True)
    inverse = lax.rsqrt(variance + EPSILON)
    return centred * inverse, inverse


def norm_back(grad_out, normed, inverse, gain_row):
    scaled = grad_out * gain_row
    inner = (
        scaled
        - jnp.mean(scaled, axis=-1, keepdims=True)
        - normed * jnp.mean(scaled * normed, axis=-1, keepdims=True)
    )
    return inner * inverse


def dot(left, right):
    return jnp.dot(left, right, preferred_element_type=f32)


def dot_t(left, right):
    return lax.dot_general(left, right, (((1,), (1,)), ((), ())), preferred_element_type=f32)


def t_dot(left, right):
    return lax.dot_general(left, right, (((0,), (0,)), ((), ())), preferred_element_type=f32)


def local(tokens, lengths, vectors, fc1_bias, w_qkv, w_dense, w_fc1, w_fc2, cotangent):
    rows, width = tokens.shape
    ax, az = lax.axis_index("x"), lax.axis_index("z")
    core, yh = lax.axis_index("c"), lax.axis_index("yh")
    part = width // 8
    ff_part = fc1_bias.shape[0]
    heads = part // HEAD_DIM
    slot = rows * 8
    scale = HEAD_DIM ** (-0.5)
    own_pos = jnp.arange(rows, dtype=jnp.int32) * 8 + ax * 2 + yh
    valid = (own_pos < lengths[0]).astype(f32)[:, None]

    tok = move(tokens)
    dm_own = move((valid * cotangent.astype(f32)).astype(bf16))
    x_all = gather_rows(tok).reshape(slot, width)

    sub = w_qkv.shape[0] // NZ

    def piece_for(step):
        member = ((ax + step) % NX) * 2 + core
        row = az * sub
        cols = [
            lax.dynamic_slice(w_qkv, (row, i * width + member * part), (sub, part)) for i in range(3)
        ]
        cols.append(lax.dynamic_slice(w_fc1, (row, member * ff_part), (sub, ff_part)))
        return jnp.concatenate(cols, 1)

    pieces = [piece_for(0)] + [along_x(piece_for(k), k) for k in (1, 2, 3)]
    by_x = jnp.zeros((NX,) + pieces[0].shape, bf16)
    for k in range(NX):
        by_x = lax.dynamic_update_slice(by_x, pieces[k][None], ((ax - k) % NX, 0, 0))
    from_y = lax.ppermute(by_x, ("yl", "yh"), [(0, 3), (1, 2), (2, 1), (3, 0)])
    by_xy = jnp.where(yh == 0, jnp.stack([by_x, from_y], 1), jnp.stack([from_y, by_x], 1))

    def over_z(block):
        cols = block.shape[-1]
        block = block.reshape(8, 1, sub, cols)
        full = jnp.zeros((8, NZ, sub, cols), bf16)
        for k in range(NZ):
            got = block if k == 0 else along_z(block, k)
            full = lax.dynamic_update_slice(full, got, (0, (az - k) % NZ, 0, 0))
        return full.reshape(width, cols)

    wq = over_z(by_xy[..., : 3 * part])
    wf1 = over_z(by_xy[..., 3 * part :])
    wd = move(w_dense)
    wf2 = move(w_fc2)
    vec_all = lax.all_gather(vectors, ("x", "yh"), axis=1, tiled=True)
    vec_part = move(vectors)
    bias_part = move(fc1_bias)

    inputs = x_all.astype(f32)
    unit_one, _ = normalize(inputs)
    a_b = (unit_one * vec_all[0] + vec_all[1]).astype(bf16)
    projected = dot(a_b, wq)
    query = (projected[:, :part] + vec_part[2]).astype(bf16)
    key = projected[:, part : 2 * part].astype(bf16)
    value = (projected[:, 2 * part :] + vec_part[3]).astype(bf16)

    steps = jnp.arange(4, dtype=jnp.int32)[:, None, None]
    others = jnp.arange(2, dtype=jnp.int32)[None, :, None]
    member = ((ax - steps) % NX) * 2 + (core ^ others)
    pos = (jnp.arange(rows, dtype=jnp.int32)[None, None, :] * 8 + member).reshape(slot)
    head = ((ax * 2 + core) * heads + jnp.arange(heads, dtype=jnp.int32)).astype(f32)
    slopes = jnp.exp2(-8.0 * (head + 1.0) / (heads * 8))
    distance = (pos[None, :] - pos[:, None]).astype(f32)
    causal = (pos[None, :] <= pos[:, None])[None]
    qh = query.reshape(slot, heads, HEAD_DIM)
    kh = key.reshape(slot, heads, HEAD_DIM)
    vh = value.reshape(slot, heads, HEAD_DIM)

    def scores():
        raw = jnp.einsum("qhd,khd->hqk", qh, kh, preferred_element_type=f32)
        return jnp.where(causal, raw * scale + slopes[:, None, None] * distance[None], -1e30)

    s = scores()
    row_max = jnp.max(s, axis=-1, keepdims=True)
    exponent = jnp.exp(s - row_max)
    total = jnp.sum(exponent, axis=-1, keepdims=True)
    lse = row_max + jnp.log(total)
    att_b = (exponent / total).astype(bf16)
    ctx_b = (
        jnp.einsum("hqk,khd->qhd", att_b, vh, preferred_element_type=f32)
        .reshape(slot, part)
        .astype(bf16)
    )
    hidden = (
        tok.astype(f32)
        + scatter_rows(dot(ctx_b, wd).reshape(4, 2, rows, width))
        + vec_all[4]
    )
    unit_two, inverse_two = normalize(hidden)
    c_own = (unit_two * vec_all[5] + vec_all[6]).astype(bf16)
    c_b = gather_rows(c_own).reshape(slot, width)
    dm = gather_rows(dm_own).reshape(slot, width)
    pre = dot(c_b, wf1) + bias_part
    activated, gelu_back = jax.vjp(lambda v: jax.nn.gelu(v, approximate=False), pre)
    act_b = activated.astype(bf16)
    d_act = dot_t(dm, wf2).astype(bf16)
    du_b = gelu_back(d_act.astype(f32))[0].astype(bf16)
    dc = scatter_rows(dot_t(du_b, wf1).reshape(4, 2, rows, width))
    out_own = hidden + scatter_rows(dot(act_b, wf2).reshape(4, 2, rows, width)) + vec_all[7]
    output = (valid * move(out_own.astype(bf16)).astype(f32)).astype(bf16)
    g_fc2 = t_dot(act_b, dm).astype(bf16)
    g_fc1 = t_dot(c_b, du_b).astype(bf16)
    dh = dm_own.astype(f32) + norm_back(dc, unit_two, inverse_two, vec_all[5])
    dh_own = dh.astype(bf16)
    dh_b = gather_rows(dh_own).reshape(slot, width)
    g_dense = t_dot(ctx_b, dh_b).astype(bf16)
    dctx = dot_t(dh_b, wd).astype(bf16).reshape(slot, heads, HEAD_DIM)

    att = jnp.exp(scores() - lse)
    d_prob = jnp.einsum("qhd,khd->hqk", dctx, vh, preferred_element_type=f32)
    inner = jnp.sum(att * d_prob, axis=-1, keepdims=True)
    ds_b = (att * (d_prob - inner)).astype(bf16)
    dq = jnp.einsum("hqk,khd->qhd", ds_b, kh, preferred_element_type=f32) * scale
    dk = jnp.einsum("hqk,qhd->khd", ds_b, qh, preferred_element_type=f32) * scale
    dv = jnp.einsum("hqk,qhd->khd", att.astype(bf16), dctx, preferred_element_type=f32)
    d_proj = jnp.concatenate([t.reshape(slot, part).astype(bf16) for t in (dq, dk, dv)], 1)
    g_qkv = t_dot(a_b, d_proj).astype(bf16)
    da = scatter_rows(dot_t(d_proj, wq).reshape(4, 2, rows, width))
    own_unit, own_inverse = normalize(tok.astype(f32))
    d_tokens = move((dh + norm_back(da, own_unit, own_inverse, vec_all[0])).astype(bf16))

    slots = ("z", "yl", "yh")
    home = yh == core

    def summed(values):
        return lax.psum(values.astype(bf16), slots)

    def rows_home(values):
        return jnp.where(home, values, across_core(values)).astype(f32)

    def columns_home(values, groups):
        cols = values.shape[1]
        mine = lax.dynamic_slice(
            values.reshape(NX, 2, part, cols), (0, yh, 0, 0), (NX, 1, part, cols)
        ).reshape(NX, part, cols)
        by_source = jnp.zeros((NX, part, cols), bf16)
        for k in range(NX):
            block = lax.dynamic_slice(mine, ((ax + k) % NX, 0, 0), (1, part, cols))
            got = block if k == 0 else along_x(block, k)
            by_source = lax.dynamic_update_slice(by_source, got, ((ax - k) % NX, 0, 0))
        theirs = across_core(by_source)
        both = jnp.where(
            core == 0, jnp.stack([by_source, theirs], 1), jnp.stack([theirs, by_source], 1)
        )
        return (
            both.reshape(8, part, groups, cols // groups)
            .transpose(1, 2, 0, 3)
            .reshape(part, 8 * cols)
            .astype(f32)
        )

    grad_fc2 = rows_home(summed(g_fc2))
    grad_fc1 = columns_home(summed(g_fc1), 1)
    grad_dense = rows_home(summed(g_dense))
    grad_qkv = columns_home(summed(g_qkv), 3)
    token_terms = jnp.stack(
        [
            jnp.sum(da * own_unit, 0),
            jnp.sum(da, 0),
            jnp.sum(dh_own.astype(f32), 0),
            jnp.sum(dc * unit_two, 0),
            jnp.sum(dc, 0),
            jnp.sum(dm_own.astype(f32), 0),
        ]
    )
    token_terms = lax.psum(token_terms.astype(bf16), ALL).astype(f32)
    token_terms = lax.dynamic_slice(token_terms, (0, (ax * 2 + yh) * part), (6, part))
    member_terms = jnp.concatenate(
        [
            jnp.sum(d_proj[:, :part].astype(f32), 0),
            jnp.sum(d_proj[:, 2 * part :].astype(f32), 0),
            jnp.sum(du_b.astype(f32), 0),
        ]
    )
    member_terms = rows_home(summed(member_terms))
    grad_vectors = jnp.concatenate(
        [token_terms[:2], member_terms[: 2 * part].reshape(2, part), token_terms[2:]]
    )
    return (
        output,
        d_tokens,
        grad_vectors,
        member_terms[2 * part :],
        grad_qkv,
        grad_dense,
        grad_fc1,
        grad_fc2,
    )


def solution(mesh):
    fine = Mesh(np.asarray(mesh.devices).reshape(4, 2, 2, 4, 2), ALL)
    rows = P(("z", "yl", "c", "x", "yh"), None)
    shard = P(("x", "yh"), None)
    return jax.shard_map(
        local,
        mesh=fine,
        in_specs=(
            rows,
            P(("z", "yl", "c")),
            P(None, ("x", "yh")),
            P(("x", "yh")),
            shard,
            shard,
            shard,
            shard,
            rows,
        ),
        out_specs=(
            rows,
            rows,
            P(None, ("x", "yh")),
            P(("x", "yh")),
            shard,
            shard,
            shard,
            shard,
        ),
        check_vma=False,
    )
```

time: 2940 us -> 880 us (0.30)
  waiting for transfers between devices: 2490 us -> 298 us
  starting transfers between devices: 0.95 us -> 144 us
  matrix products: 229 us -> 102 us
  local copies, waits for them, and re-layouts: 43.8 us -> 93.7 us
  other arithmetic: 42.4 us -> 78.7 us
    all_gather x6 -> x0, waiting for transfers between devices: 1080 us -> none  [the longest x4 974 us: project(): lax.all_gather(weight, 'shard', axis=0, tiled=True)]
    reduce_scatter x5 -> x0, waiting for transfers between devices: 1040 us -> none  [the longest x4 1030 us: weight_grad(): lax.psum_scatter(lax.dot_general(acts_b, grad_b, tokens_first, preferred_...]
    ppermute x0 -> x65, waiting for transfers between devices: none -> 180 us  [the longest x33 105 us: along_x(): return lax.ppermute(values, 'x', [(i, (i + step) % NX) for i in range(NX)])]
    ppermute x0 -> x65, starting transfers between devices: none -> 144 us  [the longest x17 55.9 us: across_core(): return lax.ppermute(values, 'c', [(0, 1), (1, 0)])]
    psum x1, waiting for transfers between devices: 261 us -> 117 us  [summed(): return lax.psum(values.astype(bf16), slots)]
    dot_general x18, matrix products: 229 us -> 102 us  [the longest x4 25.4 us: dot(): return jnp.dot(left, right, preferred_element_type=f32)]
    unnamed x16 -> x1, waiting for transfers between devices: 116 us -> 0.02 us
    psum x1 -> x2, blocking collectives: 23.8 us -> 91.4 us  [the longest x1 63.3 us: local(): token_terms = lax.psum(token_terms.astype(bf16), ALL).astype(f32)]
  transfers between devices with their start and end apart: 14 -> 66, of which waited for: 14 -> 22; matrix products, arithmetic and copies ran while one was open for 7% -> 23% of each run, Pallas kernels for 0% -> 0%
where the time goes in v1:
time: 880 us; the launch traced here: 866 us
  waiting for transfers between devices  298 us (34%)
  starting transfers between devices  144 us (16%)
  blocking collectives  133 us (15%)
  matrix products  102 us (12%)
  local copies, waits for them, and re-layouts  93.7 us (11%)
  other arithmetic  78.7 us (9%)
  between operations  16.9 us (2%)
    psum x1, waiting for transfers between devices, summed(): return lax.psum(values.astype(bf16), slots)  117 us
    ppermute x33, waiting for transfers between devices, along_x(): return lax.ppermute(values, 'x', [(i, (i + step) % NX) for i in range(NX)])  105 us
    ppermute x6, waiting for transfers between devices, along_z(): return lax.ppermute(values, 'z', [(i, (i + step) % NZ) for i in range(NZ)])  68.7 us
    psum x1, blocking collectives, local(): token_terms = lax.psum(token_terms.astype(bf16), ALL).astype(f32)  63.3 us
    ppermute x17, starting transfers between devices, across_core(): return lax.ppermute(values, 'c', [(0, 1), (1, 0)])  55.9 us
    all_gather x1, blocking collectives, local(): vec_all = lax.all_gather(vectors, ('x', 'yh'), axis=1, tiled=True)  41.3 us
    ppermute x33, starting transfers between devices, along_x(): return lax.ppermute(values, 'x', [(i, (i + step) % NX) for i in range(NX)])  37.7 us
    unnamed x151, local copies, waits for them, and re-layouts  28.9 us
  transfers between devices with their start and end apart: 66, of which 22 were waited for; matrix products, arithmetic and copies ran while one was open for 23% of the time, Pallas kernels for 0%

profile of v1, /device:TPU:63, one launch (start us, length us, event | category | flops | bytes accessed | tf_op | source)
XLA Modules:
  0.0 866.2 jit_solution(4157912743352569918)
XLA Ops:
  29.6 41.3 %all_gather.3 = f32[8,2048]{1,0:T(8,128)S(1)} all-gather(f32[8,256]{1,0:T(8,128)S(1)} %copy-done.52), channel_id=1, replica_groups=mesh['z'=4,'yl'=2,'c'=2,'x'=4,'yh'=2] {'x','yh'}, dimensions={1}, use_global_device_ids=true | all-gather | bytes 73728 | tf_op jit(solution)/shard_map/all_gather | solution.py:132
  71.5 9.5 %collective-permute-start.14 = (bf16[256,2048]{1,0:T(8,128)(2,1)}, bf16[256,2048]{1,0:T(8,128)(2,1)}, u32[]{:S(2)}, u32[]{:S(2)}) collective-permute-start(bf16[256,2048]{1,0:T(8,128)(2,1)} %param.14), channel_id=1, source_target_pairs={{0,0},{1,8},{8,1},{9,9},{2,2},{3,10},{10,3},{11,11},{4,4},{5,12},{... | collective-permute-start | bytes 3145736 | tf_op jit(solution)/shard_map/ppermute | solution.py:19
  94.7 12.2 %collective-permute-done.10 = bf16[8,1,64,768]{3,2,0,1:T(8,128)(2,1)} collective-permute-done((bf16[8,1,64,768]{3,2,0,1:T(8,128)(2,1)S(1)}, bf16[8,1,64,768]{3,2,0,1:T(8,128)(2,1)}, u32[]{:S(2)}, u32[]{:S(2)}) %collective-permute-start.10) | collective-permute-done | bytes 786464 | tf_op jit(solution)/shard_map/ppermute | solution.py:31
  110.0 17.0 %collective-permute-done.12 = bf16[8,1,64,768]{3,2,0,1:T(8,128)(2,1)S(1)} collective-permute-done((bf16[8,1,64,768]{3,2,0,1:T(8,128)(2,1)S(1)}, bf16[8,1,64,768]{3,2,0,1:T(8,128)(2,1)S(1)}, u32[]{:S(2)}, u32[]{:S(2)}) %collective-permute-start.12) | collective-permute-done | bytes 786464 | tf_op jit(solution)/shard_map/ppermute | solution.py:31
  156.9 8.6 fusion.46
  172.6 14.1 %collective-permute-start.35 = (bf16[128,2048]{1,0:T(8,128)(2,1)S(1)}, bf16[128,2048]{1,0:T(8,128)(2,1)S(1)}, u32[]{:S(2)}, u32[]{:S(2)}) collective-permute-start(bf16[128,2048]{1,0:T(8,128)(2,1)S(1)} %collective-permute-done.34), channel_id=1, source_target_pairs={{0,8},{8,0},{1,9},{9,1},{2,10},{10,2},{3,11},{11,3},{4,12},{12,4},... | collective-permute-start | bytes 1572872 | tf_op jit(solution)/shard_map/ppermute | solution.py:23
  191.3 20.3 %collective-permute-done.36 = bf16[128,2048]{1,0:T(8,128)(2,1)S(1)} collective-permute-done((bf16[128,2048]{1,0:T(8,128)(2,1)S(1)}, bf16[128,2048]{1,0:T(8,128)(2,1)S(1)}, u32[]{:S(2)}, u32[]{:S(2)}) %collective-permute-start.36) | collective-permute-done | bytes 524320 | tf_op jit(solution)/shard_map/ppermute | solution.py:27
  221.5 18.5 %collective-permute-done.24 = bf16[8,1,64,1024]{3,2,0,1:T(8,128)(2,1)} collective-permute-done((bf16[8,1,64,1024]{3,2,0,1:T(8,128)(2,1)S(1)}, bf16[8,1,64,1024]{3,2,0,1:T(8,128)(2,1)}, u32[]{:S(2)}, u32[]{:S(2)}) %collective-permute-start.24) | collective-permute-done | bytes 1048608 | tf_op jit(solution)/shard_map/ppermute | solution.py:31
  246.8 21.3 %collective-permute-start.26 = (bf16[8,1,64,1024]{3,2,0,1:T(8,128)(2,1)S(1)}, bf16[8,1,64,1024]{3,2,0,1:T(8,128)(2,1)S(1)}, u32[]{:S(2)}, u32[]{:S(2)}) collective-permute-start(bf16[8,1,64,1024]{3,2,0,1:T(8,128)(2,1)S(1)} %bitcast.316), channel_id=1, source_target_pairs={{0,96},{32,0},{64,32},{96,64},{1,97},{33,1},{65,33},{97,65},{2,98}... | collective-permute-start | bytes 3145736 | tf_op jit(solution)/shard_map/ppermute | solution.py:31
  271.4 19.3 %collective-permute-done.26 = bf16[8,1,64,1024]{3,2,0,1:T(8,128)(2,1)S(1)} collective-permute-done((bf16[8,1,64,1024]{3,2,0,1:T(8,128)(2,1)S(1)}, bf16[8,1,64,1024]{3,2,0,1:T(8,128)(2,1)S(1)}, u32[]{:S(2)}, u32[]{:S(2)}) %collective-permute-start.26) | collective-permute-done | bytes 1048608 | tf_op jit(solution)/shard_map/ppermute | solution.py:31
  292.7 12.1 %collective-permute-done.22 = bf16[128,2048]{1,0:T(8,128)(2,1)S(1)} collective-permute-done((bf16[128,2048]{1,0:T(8,128)(2,1)S(1)}, bf16[128,2048]{1,0:T(8,128)(2,1)S(1)}, u32[]{:S(2)}, u32[]{:S(2)}) %collective-permute-start.22) | collective-permute-done | bytes 524320 | tf_op jit(solution)/shard_map/ppermute | solution.py:27
  311.8 14.5 %multiply_convert_fusion.1 = (bf16[1024,1024]{1,0:T(8,128)(2,1)S(1)}, f32[1024,1024]{1,0:T(8,128)}, f32[1024,1024]{1,0:T(8,128)}) fusion(f32[1024]{0:T(1024)S(1)} %collective-permute-done.27, bf16[1024,2048]{1,0:T(8,128)(2,1)S(1)} %bitcast.319, bf16[2048,1024]{1,0:T(8,128)(2,1)S(1)} %bitcast.323), kind=kOutput, calls=%fused_computation.50 | convolution fusion | flops 4364173312 | bytes 18878464 | tf_op jit(solution)/shard_map/dot_general | solution.py:74
  336.0 17.8 %collective-permute-start.29 = (bf16[4,128,2048]{2,1,0:T(8,128)(2,1)}, bf16[4,128,2048]{2,1,0:T(8,128)(2,1)}, u32[]{:S(2)}, u32[]{:S(2)}) collective-permute-start(bf16[4,128,2048]{2,1,0:T(8,128)(2,1)} %fusion.31), channel_id=1, source_target_pairs={{0,8},{8,0},{1,9},{9,1},{2,10},{10,2},{3,11},{11,3},{4,12},{12,4},... | collective-permute-start | bytes 6291464 | tf_op jit(solution)/shard_map/ppermute | solution.py:23
  353.7 8.8 %fusion.108 = (bf16[1024]{0:T(1024)(128)(2,1)}, bf16[1024,1024]{1,0:T(8,128)(2,1)S(1)}) fusion(f32[1024,1024]{1,0:T(8,128)S(1)} %copy-done.69, bf16[1024,2048]{1,0:T(8,128)(2,1)S(1)} %bitcast.317, bf16[1024,2048]{1,0:T(8,128)(2,1)S(1)} %copy-done.63, f32[1024,1024]{1,0:T(8,128)} %get-tuple-element.115, f32[1024]{0:T(1024)S(1)} %collective-permute-done.27), kind=kOutput, calls=%fused_computation.253 | convolution fusion | flops 4313840640 | bytes 18880512 | tf_op jit(solution)/shard_map/dot_general | solution.py:78
  390.8 11.2 %collective-permute-done.31 = bf16[128,2048]{1,0:T(8,128)(2,1)S(1)} collective-permute-done((bf16[128,2048]{1,0:T(8,128)(2,1)}, bf16[128,2048]{1,0:T(8,128)(2,1)S(1)}, u32[]{:S(2)}, u32[]{:S(2)}) %collective-permute-start.31) | collective-permute-done | bytes 524320 | tf_op jit(solution)/shard_map/ppermute | solution.py:27
  402.0 10.7 %collective-permute-done.41 = bf16[128,2048]{1,0:T(8,128)(2,1)S(1)} collective-permute-done((bf16[128,2048]{1,0:T(8,128)(2,1)S(1)}, bf16[128,2048]{1,0:T(8,128)(2,1)S(1)}, u32[]{:S(2)}, u32[]{:S(2)}) %collective-permute-start.41) | collective-permute-done | bytes 524320 | tf_op jit(solution)/shard_map/ppermute | solution.py:27
  412.7 11.5 %collective-permute-done.42 = bf16[128,2048]{1,0:T(8,128)(2,1)S(1)} collective-permute-done((bf16[128,2048]{1,0:T(8,128)(2,1)S(1)}, bf16[128,2048]{1,0:T(8,128)(2,1)S(1)}, u32[]{:S(2)}, u32[]{:S(2)}) %collective-permute-start.42) | collective-permute-done | bytes 524320 | tf_op jit(solution)/shard_map/ppermute | solution.py:27
  443.4 9.7 %collective-permute-done.47 = bf16[128,2048]{1,0:T(8,128)(2,1)S(1)} collective-permute-done((bf16[128,2048]{1,0:T(8,128)(2,1)S(1)}, bf16[128,2048]{1,0:T(8,128)(2,1)S(1)}, u32[]{:S(2)}, u32[]{:S(2)}) %collective-permute-start.47) | collective-permute-done | bytes 524320 | tf_op jit(solution)/shard_map/ppermute | solution.py:27
  541.2 28.1 %psum.43 = bf16[1536]{0:T(1024)(128)(2,1)} all-reduce(bf16[1536]{0:T(1024)(128)(2,1)S(1)} %pad_maximum_fusion.13), channel_id=1, replica_groups=mesh['z'=4,'yl'=2,'c'=2,'x'=4,'yh'=2] {'z','yl','yh'}, use_global_device_ids=true, to_apply=%region_23.24 | all-reduce | flops 1536 | bytes 6144 | tf_op jit(solution)/shard_map/psum | solution.py:213
  572.2 117.5 %all-reduce.3.cloned.1.call-done = (bf16[4,2,256,768]{3,2,1,0:T(8,128)(2,1)}, bf16[256,2048]{1,0:T(8,128)(2,1)}, bf16[4,2,256,1024]{3,2,1,0:T(8,128)(2,1)}, bf16[1024,2048]{1,0:T(8,128)(2,1)}) async-done(((bf16[4,2,256,768]{3,2,1,0:T(8,128)(2,1)}, bf16[256,2048]{1,0:T(8,128)(2,1)}, bf16[4,2,256,1024]{3,2,1,0:T(8,128)(2,1)}, bf16[1024,2048]{1,0:T(8,128)(2,1)}), (bf16[4,2,256,768]{3,2,1,0:T(8,128)(2,1)}, ...) | async-done | bytes 12582928 | tf_op jit(solution)/shard_map/psum | solution.py:213
  721.6 8.3 collective-permute-start.54
  745.9 63.3 %psum.42 = bf16[6,2048]{1,0:T(8,128)(2,1)S(1)} all-reduce(bf16[6,2048]{1,0:T(8,128)(2,1)S(1)} %stack.332), channel_id=1, replica_groups=mesh['z'=4,'yl'=2,'c'=2,'x'=4,'yh'=2] {'z','yl','c','x','yh'}, use_global_device_ids=true, to_apply=%region_19.20 | all-reduce | flops 12288 | bytes 49152 | tf_op jit(solution)/shard_map/psum | solution.py:253
  832.9 9.2 %copy.116 = f32[256,1,8,1024]{0,3,2,1:T(8,128)} copy(f32[256,1,8,1024]{3,0,2,1:T(8,128)} %bitcast.303) | data formatting | bytes 16777216 | tf_op jit(solution)/shard_map/convert_element_type | solution.py:236
  842.0 8.9 %copy.118 = f32[256,8192]{1,0:T(8,128)} copy(f32[256,8192]{0,1:T(8,128)} %bitcast.304) | data formatting | bytes 16777216
  (432 shorter events, 335.8 us)
Async XLA Ops:
  7.2 682.5 %all-reduce.3.cloned.1.call-start = ((), (), s32[]{:S(2)}) async-start(), calls=%async_computation | async-start | bytes 25165824 | tf_op jit(solution)/shard_map/psum | solution.py:213
  13.8 76.1 %collective-permute-start.13 = (f32[8,256]{1,0:T(8,128)}, f32[8,256]{1,0:T(8,128)S(1)}, u32[]{:S(2)}, u32[]{:S(2)}) collective-permute-start(f32[8,256]{1,0:T(8,128)} %param.11), channel_id=1, source_target_pairs={{0,0},{1,8},{8,1},{9,9},{2,2},{3,10},{10,3},{11,11},{4,4},{5,12},{... | collective-permute-start | bytes 24584 | tf_op jit(solution)/shard_map/ppermute | solution.py:19
  23.8 61.3 %collective-permute-start.9 = (bf16[4,64,1792]{2,1,0:T(8,128)(2,1)S(1)}, bf16[4,64,1792]{2,1,0:T(8,128)(2,1)}, u32[]{:S(2)}, u32[]{:S(2)}) collective-permute-start(bf16[4,64,1792]{2,1,0:T(8,128)(2,1)S(1)} %bitcast_dynamic-update-slice_fusion.8), channel_id=1, source_target_pairs={{0,17},{1,16},{16,1},{17,0},{2,19},{3,18},{18,3},{19,2},{4,21},{5,... | collective-permute-start | bytes 2752520 | tf_op jit(solution)/shard_map/ppermute | solution.py:116
  24.0 47.6 %collective-permute-start.2 = (bf16[128,2048]{1,0:T(8,128)(2,1)S(1)}, bf16[128,2048]{1,0:T(8,128)(2,1)S(1)}, u32[]{:S(2)}, u32[]{:S(2)}) collective-permute-start(bf16[128,2048]{1,0:T(8,128)(2,1)S(1)} %collective-permute-done), channel_id=1, source_target_pairs={{0,2},{2,4},{4,6},{6,0},{1,3},{3,5},{5,7},{7,1},{8,10},{10,12},{12... | collective-permute-start | bytes 1572872 | tf_op jit(solution)/shard_map/ppermute | solution.py:27
  25.8 55.2 %collective-permute-start.3 = (bf16[128,2048]{1,0:T(8,128)(2,1)S(1)}, bf16[128,2048]{1,0:T(8,128)(2,1)S(1)}, u32[]{:S(2)}, u32[]{:S(2)}) collective-permute-start(bf16[128,2048]{1,0:T(8,128)(2,1)S(1)} %collective-permute-done), channel_id=1, source_target_pairs={{0,6},{2,0},{4,2},{6,4},{1,7},{3,1},{5,3},{7,5},{8,14},{10,8},{12,... | collective-permute-start | bytes 1572872 | tf_op jit(solution)/shard_map/ppermute | solution.py:27
  25.8 57.9 %collective-permute-start.4 = (bf16[128,2048]{1,0:T(8,128)(2,1)S(1)}, bf16[128,2048]{1,0:T(8,128)(2,1)S(1)}, u32[]{:S(2)}, u32[]{:S(2)}) collective-permute-start(bf16[128,2048]{1,0:T(8,128)(2,1)S(1)} %collective-permute-done), channel_id=1, source_target_pairs={{0,4},{2,6},{4,0},{6,2},{1,5},{3,7},{5,1},{7,3},{8,12},{10,14},{12... | collective-permute-start | bytes 1572872 | tf_op jit(solution)/shard_map/ppermute | solution.py:27
  71.5 96.1 %collective-permute-start.14 = (bf16[256,2048]{1,0:T(8,128)(2,1)}, bf16[256,2048]{1,0:T(8,128)(2,1)}, u32[]{:S(2)}, u32[]{:S(2)}) collective-permute-start(bf16[256,2048]{1,0:T(8,128)(2,1)} %param.14), channel_id=1, source_target_pairs={{0,0},{1,8},{8,1},{9,9},{2,2},{3,10},{10,3},{11,11},{4,4},{5,12},{... | collective-permute-start | bytes 3145736 | tf_op jit(solution)/shard_map/ppermute | solution.py:19
  85.1 42.0 %collective-permute-start.5 = (bf16[3,128,2048]{2,1,0:T(8,128)(2,1)}, bf16[3,128,2048]{2,1,0:T(8,128)(2,1)}, u32[]{:S(2)}, u32[]{:S(2)}) collective-permute-start(bf16[3,128,2048]{2,1,0:T(8,128)(2,1)} %pad_maximum_fusion.4), channel_id=1, source_target_pairs={{0,8},{8,0},{1,9},{9,1},{2,10},{10,2},{3,11},{11,3},{4,12},{12,4},... | collective-permute-start | bytes 4718600 | tf_op jit(solution)/shard_map/ppermute | solution.py:23
  91.1 35.9 %collective-permute-start.12 = (bf16[8,1,64,768]{3,2,0,1:T(8,128)(2,1)S(1)}, bf16[8,1,64,768]{3,2,0,1:T(8,128)(2,1)S(1)}, u32[]{:S(2)}, u32[]{:S(2)}) collective-permute-start(bf16[8,1,64,768]{3,2,0,1:T(8,128)(2,1)S(1)} %bitcast.328), channel_id=1, source_target_pairs={{0,96},{32,0},{64,32},{96,64},{1,97},{33,1},{65,33},{97,65},{2,98}... | collective-permute-start | bytes 2359304 | tf_op jit(solution)/shard_map/ppermute | solution.py:31
  170.7 48.5 %collective-permute-start.15 = (bf16[4,128,2048]{2,1,0:T(8,128)(2,1)S(1)}, bf16[4,128,2048]{2,1,0:T(8,128)(2,1)S(1)}, u32[]{:S(2)}, u32[]{:S(2)}) collective-permute-start(bf16[4,128,2048]{2,1,0:T(8,128)(2,1)S(1)} %fusion.28), channel_id=1, source_target_pairs={{0,8},{8,0},{1,9},{9,1},{2,10},{10,2},{3,11},{11,3},{4,12},{12,4},... | collective-permute-start | bytes 6291464 | tf_op jit(solution)/shard_map/ppermute | solution.py:23
  190.5 121.3 %collective-permute-start.27 = (f32[1024]{0:T(1024)S(1)}, f32[1024]{0:T(1024)S(1)}, u32[]{:S(2)}, u32[]{:S(2)}) collective-permute-start(f32[1024]{0:T(1024)S(1)} %copy-done.64), channel_id=1, source_target_pairs={{0,0},{1,8},{8,1},{9,9},{2,2},{3,10},{10,3},{11,11},{4,4},{5,12},{... | collective-permute-start | bytes 12296 | tf_op jit(solution)/shard_map/ppermute | solution.py:19
  221.1 47.0 %collective-permute-start.17 = (bf16[128,2048]{1,0:T(8,128)(2,1)S(1)}, bf16[128,2048]{1,0:T(8,128)(2,1)S(1)}, u32[]{:S(2)}, u32[]{:S(2)}) collective-permute-start(bf16[128,2048]{1,0:T(8,128)(2,1)S(1)} %get-tuple-element.89), channel_id=1, source_target_pairs={{0,6},{2,0},{4,2},{6,4},{1,7},{3,1},{5,3},{7,5},{8,14},{10,8},{12,... | collective-permute-start | bytes 1572872 | tf_op jit(solution)/shard_map/ppermute | solution.py:27
  242.2 49.3 %collective-permute-start.39 = (bf16[3,128,2048]{2,1,0:T(8,128)(2,1)S(1)}, bf16[3,128,2048]{2,1,0:T(8,128)(2,1)S(1)}, u32[]{:S(2)}, u32[]{:S(2)}) collective-permute-start(bf16[3,128,2048]{2,1,0:T(8,128)(2,1)S(1)} %copy-done.37), channel_id=1, source_target_pairs={{0,8},{8,0},{1,9},{9,1},{2,10},{10,2},{3,11},{11,3},{4,12},{12,4},... | collective-permute-start | bytes 4718600 | tf_op jit(solution)/shard_map/ppermute | solution.py:23
  246.8 43.9 %collective-permute-start.26 = (bf16[8,1,64,1024]{3,2,0,1:T(8,128)(2,1)S(1)}, bf16[8,1,64,1024]{3,2,0,1:T(8,128)(2,1)S(1)}, u32[]{:S(2)}, u32[]{:S(2)}) collective-permute-start(bf16[8,1,64,1024]{3,2,0,1:T(8,128)(2,1)S(1)} %bitcast.316), channel_id=1, source_target_pairs={{0,96},{32,0},{64,32},{96,64},{1,97},{33,1},{65,33},{97,65},{2,98}... | collective-permute-start | bytes 3145736 | tf_op jit(solution)/shard_map/ppermute | solution.py:31
  291.5 34.9 %collective-permute-start.28 = (bf16[1024,2048]{1,0:T(8,128)(2,1)S(1)}, bf16[1024,2048]{1,0:T(8,128)(2,1)S(1)}, u32[]{:S(2)}, u32[]{:S(2)}) collective-permute-start(bf16[1024,2048]{1,0:T(8,128)(2,1)S(1)} %copy-done.61), channel_id=1, source_target_pairs={{0,0},{1,8},{8,1},{9,9},{2,2},{3,10},{10,3},{11,11},{4,4},{5,12},{... | collective-permute-start | bytes 12582920 | tf_op jit(solution)/shard_map/ppermute | solution.py:19
  336.0 34.1 %collective-permute-start.29 = (bf16[4,128,2048]{2,1,0:T(8,128)(2,1)}, bf16[4,128,2048]{2,1,0:T(8,128)(2,1)}, u32[]{:S(2)}, u32[]{:S(2)}) collective-permute-start(bf16[4,128,2048]{2,1,0:T(8,128)(2,1)} %fusion.31), channel_id=1, source_target_pairs={{0,8},{8,0},{1,9},{9,1},{2,10},{10,2},{3,11},{11,3},{4,12},{12,4},... | collective-permute-start | bytes 6291464 | tf_op jit(solution)/shard_map/ppermute | solution.py:23
  382.9 41.3 %collective-permute-start.42 = (bf16[128,2048]{1,0:T(8,128)(2,1)S(1)}, bf16[128,2048]{1,0:T(8,128)(2,1)S(1)}, u32[]{:S(2)}, u32[]{:S(2)}) collective-permute-start(bf16[128,2048]{1,0:T(8,128)(2,1)S(1)} %get-tuple-element.83), channel_id=1, source_target_pairs={{0,6},{2,0},{4,2},{6,4},{1,7},{3,1},{5,3},{7,5},{8,14},{10,8},{12,... | collective-permute-start | bytes 1572872 | tf_op jit(solution)/shard_map/ppermute | solution.py:27
  390.2 34.0 %collective-permute-start.43 = (bf16[128,2048]{1,0:T(8,128)(2,1)S(1)}, bf16[128,2048]{1,0:T(8,128)(2,1)S(1)}, u32[]{:S(2)}, u32[]{:S(2)}) collective-permute-start(bf16[128,2048]{1,0:T(8,128)(2,1)S(1)} %get-tuple-element.82), channel_id=1, source_target_pairs={{0,2},{2,4},{4,6},{6,0},{1,3},{3,5},{5,7},{7,1},{8,10},{10,12},{12... | collective-permute-start | bytes 1572872 | tf_op jit(solution)/shard_map/ppermute | solution.py:27
  534.7 34.5 %collective-permute-start.50 = (bf16[128,2048]{1,0:T(8,128)(2,1)S(1)}, bf16[128,2048]{1,0:T(8,128)(2,1)}, u32[]{:S(2)}, u32[]{:S(2)}) collective-permute-start(bf16[128,2048]{1,0:T(8,128)(2,1)S(1)} %get-tuple-element.78), channel_id=1, source_target_pairs={{0,4},{2,6},{4,0},{6,2},{1,5},{3,7},{5,1},{7,3},{8,12},{10,14},{12... | collective-permute-start | bytes 1572872 | tf_op jit(solution)/shard_map/ppermute | solution.py:27
  689.7 161.2 %collective-permute-start.64 = (bf16[1024,2048]{1,0:T(8,128)(2,1)}, bf16[1024,2048]{1,0:T(8,128)(2,1)}, u32[]{:S(2)}, u32[]{:S(2)}) collective-permute-start(bf16[1024,2048]{1,0:T(8,128)(2,1)} %get-tuple-element.35), channel_id=1, source_target_pairs={{0,8},{8,0},{1,9},{9,1},{2,10},{10,2},{3,11},{11,3},{4,12},{12,4},... | collective-permute-start | bytes 12582920 | tf_op jit(solution)/shard_map/ppermute | solution.py:23
  731.1 78.8 %collective-permute-start.59 = (bf16[256,2048]{1,0:T(8,128)(2,1)S(1)}, bf16[256,2048]{1,0:T(8,128)(2,1)}, u32[]{:S(2)}, u32[]{:S(2)}) collective-permute-start(bf16[256,2048]{1,0:T(8,128)(2,1)S(1)} %copy-done.38), channel_id=1, source_target_pairs={{0,8},{8,0},{1,9},{9,1},{2,10},{10,2},{3,11},{11,3},{4,12},{12,4},... | collective-permute-start | bytes 3145736 | tf_op jit(solution)/shard_map/ppermute | solution.py:23
  735.5 75.8 %collective-permute-start.58 = (bf16[4,256,768]{1,2,0:T(8,128)(2,1)}, bf16[4,256,768]{1,2,0:T(8,128)(2,1)}, u32[]{:S(2)}, u32[]{:S(2)}) collective-permute-start(bf16[4,256,768]{1,2,0:T(8,128)(2,1)} %constant_dynamic-update-slice_fusion.3), channel_id=1, source_target_pairs={{0,8},{8,0},{1,9},{9,1},{2,10},{10,2},{3,11},{11,3},{4,12},{12,4},... | collective-permute-start | bytes 4718600 | tf_op jit(solution)/shard_map/ppermute | solution.py:23
  736.8 73.1 %collective-permute-start.53 = (bf16[128,2048]{1,0:T(8,128)(2,1)}, bf16[128,2048]{1,0:T(8,128)(2,1)}, u32[]{:S(2)}, u32[]{:S(2)}) collective-permute-start(bf16[128,2048]{1,0:T(8,128)(2,1)} %fusion.56), channel_id=1, source_target_pairs={{0,0},{1,8},{8,1},{9,9},{2,2},{3,10},{10,3},{11,11},{4,4},{5,12},{... | collective-permute-start | bytes 1572872 | tf_op jit(solution)/shard_map/ppermute | solution.py:19
  742.2 83.4 %collective-permute-start.63 = (bf16[4,256,1024]{2,1,0:T(8,128)(2,1)S(1)}, bf16[4,256,1024]{2,1,0:T(8,128)(2,1)}, u32[]{:S(2)}, u32[]{:S(2)}) collective-permute-start(bf16[4,256,1024]{2,1,0:T(8,128)(2,1)S(1)} %constant_dynamic-update-slice_fusion.2), channel_id=1, source_target_pairs={{0,8},{8,0},{1,9},{9,1},{2,10},{10,2},{3,11},{11,3},{4,12},{12,4},... | collective-permute-start | bytes 6291464 | tf_op jit(solution)/shard_map/ppermute | solution.py:23
  (116 other events, 2206.4 us)
Sparse Core Ops, SparseCore 0:
  509.4 180.2 all-reduce.2

commit v2 on v1

v2 whole, which is shorter than its diff:
```python
import functools

import numpy as np
import jax
import jax.numpy as jnp
from jax import lax
from jax.experimental import pallas as pl
from jax.experimental.pallas import tpu as pltpu
from jax.sharding import Mesh
from jax.sharding import PartitionSpec as P

HEAD_DIM = 64
EPSILON = 1e-05
bf16 = jnp.bfloat16
f32 = jnp.float32

ALL = ("z", "yl", "c", "x", "yh")
NX, NZ = 4, 4
SWAP = [(1, 2), (2, 1)]


def move(values):
    got = lax.ppermute(values, ("c", "yh"), SWAP)
    return jnp.where(lax.axis_index("c") == lax.axis_index("yh"), values, got)


def move_late(values, after):
    got = gate([lax.ppermute(values, ("c", "yh"), SWAP)], after)[0]
    return jnp.where(lax.axis_index("c") == lax.axis_index("yh"), values, got)


def across_core(values):
    return lax.ppermute(values, "c", [(0, 1), (1, 0)])


def along_x(values, step):
    return lax.ppermute(values, "x", [(i, (i + step) % NX) for i in range(NX)])


def along_z(values, step):
    return lax.ppermute(values, "z", [(i, (i + step) % NZ) for i in range(NZ)])


def along_y(values, flip_yl, flip_yh):
    pairs = [(i, i ^ (2 * flip_yl + flip_yh)) for i in range(4)]
    return lax.ppermute(values, ("yl", "yh"), pairs)


def gather_rows(block):
    mine = {0: block}
    for k in (1, 3, 2):
        mine[k] = along_x(block, k)
    theirs = {k: across_core(mine[k]) for k in (0, 1, 3, 2)}
    return [part[k] for k in range(NX) for part in (mine, theirs)]


def where_blocks():
    ax, core = lax.axis_index("x"), lax.axis_index("c")
    return jnp.stack(
        [(core ^ r) * NX + (ax - k) % NX for k in range(NX) for r in range(2)]
    ).astype(jnp.int32)


def gate(values, after):
    anywhere = pl.BlockSpec(memory_space=pl.ANY)
    out = pl.pallas_call(
        lambda *refs: None,
        in_specs=[anywhere] * (len(values) + len(after)),
        out_specs=[anywhere] * len(values),
        out_shape=[jax.ShapeDtypeStruct(v.shape, v.dtype) for v in values],
        input_output_aliases={i: i for i in range(len(values))},
        cost_estimate=cost(0),
        name="gate",
    )(*values, *after)
    return list(out)


def cost(us):
    return pl.CostEstimate(flops=int(us * 1e9), bytes_accessed=int(us * 3.2e6), transcendentals=0)


def kernel_params(mib=56):
    return pltpu.CompilerParams(vmem_limit_bytes=mib << 20)


def theirs_kernel(info_ref, left_ref, right_ref, out_ref, *, contract):
    rows = left_ref.shape[1]
    out_ref[...] = lax.dot_general(
        left_ref[...].reshape(NX * rows, left_ref.shape[2]),
        right_ref[...],
        contract,
        preferred_element_type=f32,
    ).astype(out_ref.dtype)


def mine_kernel(info_ref, left_ref, right_ref, got_ref, *refs, contract):
    outs, sum_ref = refs[:NX], refs[NX]
    rows = left_ref.shape[1]
    sum_ref[...] = lax.dot_general(
        left_ref[...].reshape(NX * rows, left_ref.shape[2]),
        right_ref[...],
        contract,
        preferred_element_type=f32,
    ) + got_ref[...].astype(f32)
    for k in range(NX):
        at = pl.ds(pl.multiple_of(info_ref[1 + k] * rows, rows), rows)
        outs[k][...] = sum_ref[at, :].astype(outs[k].dtype)


def group_info():
    ax, core = lax.axis_index("x"), lax.axis_index("c")
    return jnp.stack([core] + [(ax - k) % NX for k in range(NX)]).astype(jnp.int32)


def right_side(right, transposed, tile):
    if transposed:
        return right.shape[0], pl.BlockSpec((tile, right.shape[1]), lambda n, info: (n, 0))
    return right.shape[1], pl.BlockSpec((right.shape[0], tile), lambda n, info: (0, n))


def theirs_part(left, right, transposed, name, tile=512):
    rows, depth = left.shape[1:]
    width, right_spec = right_side(right, transposed, tile)
    contract = (((1,), (1 if transposed else 0,)), ((), ()))
    sent = pl.pallas_call(
        functools.partial(theirs_kernel, contract=contract),
        grid_spec=pltpu.PrefetchScalarGridSpec(
            num_scalar_prefetch=1,
            grid=(width // tile,),
            in_specs=[
                pl.BlockSpec((NX, rows, depth), lambda n, info: (1 - info[0], 0, 0)),
                right_spec,
            ],
            out_specs=pl.BlockSpec((NX * rows, tile), lambda n, info: (0, n)),
        ),
        out_shape=jax.ShapeDtypeStruct((NX * rows, width), bf16),
        compiler_params=kernel_params(),
        cost_estimate=cost(5.0 if depth < 512 else 6.5),
        name=name + "_theirs",
    )(group_info(), left, right)
    return across_core(sent)


def mine_part(left, right, got, transposed, name, tile=512):
    rows, depth = left.shape[1:]
    width, right_spec = right_side(right, transposed, tile)
    contract = (((1,), (1 if transposed else 0,)), ((), ()))
    return pl.pallas_call(
        functools.partial(mine_kernel, contract=contract),
        grid_spec=pltpu.PrefetchScalarGridSpec(
            num_scalar_prefetch=1,
            grid=(width // tile,),
            in_specs=[
                pl.BlockSpec((NX, rows, depth), lambda n, info: (info[0], 0, 0)),
                right_spec,
                pl.BlockSpec((NX * rows, tile), lambda n, info: (0, n)),
            ],
            out_specs=[pl.BlockSpec((rows, tile), lambda n, info: (0, n))] * NX,
            scratch_shapes=[pltpu.VMEM((NX * rows, tile), f32)],
        ),
        out_shape=[jax.ShapeDtypeStruct((rows, width), f32 if k == 0 else bf16) for k in range(NX)],
        compiler_params=kernel_params(),
        cost_estimate=cost(5.4 if depth < 512 else 7.0),
        name=name + "_mine",
    )(group_info(), left, right, got)


def send_chips(chips):
    return [chips[0]] + [along_x(chips[k], -k) for k in (2, 1, 3)]


def scatter_rows(left, right, transposed, name):
    got = theirs_part(left, right, transposed, name)
    return send_chips(mine_part(left, right, got, transposed, name))


def total(terms):
    result = terms[0]
    for term in terms[1:]:
        result = result + term.astype(f32)
    return result


def row_call(kernel, blocks, fixed, per_row, outs, name, us):
    whole = lambda v: pl.BlockSpec(v.shape, lambda i, at, nd=len(v.shape): (0,) * nd)
    return pl.pallas_call(
        kernel,
        grid_spec=pltpu.PrefetchScalarGridSpec(
            num_scalar_prefetch=1,
            grid=(1,),
            in_specs=[whole(v) for v in blocks + fixed + per_row],
            out_specs=[whole(v) for v in outs],
        ),
        out_shape=outs,
        compiler_params=kernel_params(),
        cost_estimate=cost(us),
        name=name,
    )(where_blocks(), *blocks, *fixed, *per_row)


def collect_kernel(at_ref, *refs):
    for i in range(8):
        refs[8][at_ref[i]] = refs[i][...]


def pair_of(refs, k):
    return jnp.concatenate([refs[2 * k][...], refs[2 * k + 1][...]], 0)


def put_pair(ref, at_ref, k, values):
    rows = ref.shape[1]
    for r in range(2):
        ref[at_ref[2 * k + r]] = values[r * rows : (r + 1) * rows]


def norm_kernel(at_ref, *refs):
    blocks, (gain_ref, a_ref) = refs[:8], refs[8:]
    for i in range(8):
        unit, _ = normalize(blocks[i][...].astype(f32))
        a_ref[at_ref[i]] = (unit * gain_ref[0:1, :] + gain_ref[1:2, :]).astype(bf16)


def qkv_kernel(a_ref, weight_ref, bias_ref, qkv_ref):
    blocks, rows, depth = a_ref.shape
    out = jnp.dot(
        a_ref[...].reshape(blocks * rows, depth), weight_ref[...], preferred_element_type=f32
    )
    qkv_ref[...] = (out + bias_ref[...]).astype(bf16).reshape(blocks, rows, out.shape[1])


def project_qkv(a_b, weight, bias):
    blocks, rows, depth = a_b.shape
    cols, step = weight.shape[1], 2
    return pl.pallas_call(
        qkv_kernel,
        grid=(blocks // step,),
        in_specs=[
            pl.BlockSpec((step, rows, depth), lambda i: (i, 0, 0)),
            pl.BlockSpec(weight.shape, lambda i: (0, 0)),
            pl.BlockSpec(bias.shape, lambda i: (0, 0)),
        ],
        out_specs=pl.BlockSpec((step, rows, cols), lambda i: (i, 0, 0)),
        out_shape=jax.ShapeDtypeStruct((blocks, rows, cols), bf16),
        compiler_params=kernel_params(),
        cost_estimate=cost(7.0),
        name="qkv",
    )(a_b, weight, bias)


def mlp_kernel(at_ref, *refs):
    blocks, (weight_ref, bias_ref, d_act_ref, c_ref, act_ref, du_ref, sum_ref) = refs[:8], refs[8:]
    sums = jnp.zeros(sum_ref.shape, f32)
    for k in range(NX):
        c = pair_of(blocks, k)
        put_pair(c_ref, at_ref, k, c)
        pre = jnp.dot(c, weight_ref[...], preferred_element_type=f32) + bias_ref[...]
        share = 0.5 + 0.5 * lax.erf(pre * (0.5**0.5))
        put_pair(act_ref, at_ref, k, (pre * share).astype(bf16))
        slope = share + pre * (jnp.exp(-0.5 * pre * pre) * ((2.0 * np.pi) ** -0.5))
        d_act = jnp.concatenate([d_act_ref[at_ref[2 * k]], d_act_ref[at_ref[2 * k + 1]]], 0)
        du = (d_act.astype(f32) * slope).astype(bf16)
        put_pair(du_ref, at_ref, k, du)
        sums = sums + jnp.sum(du.astype(f32), axis=0, keepdims=True)
    sum_ref[...] = sums


def ctx_back_kernel(at_ref, *refs):
    blocks, (weight_ref, dh_ref, out_ref) = refs[:8], refs[8:]
    for k in range(NX):
        dh = pair_of(blocks, k)
        put_pair(dh_ref, at_ref, k, dh)
        out = lax.dot_general(
            dh, weight_ref[...], (((1,), (1,)), ((), ())), preferred_element_type=f32
        )
        put_pair(out_ref, at_ref, k, out.astype(bf16))


def normalize(values):
    average = jnp.mean(values, axis=-1, keepdims=True)
    centred = values - average
    variance = jnp.mean(centred * centred, axis=-1, keepdims=True)
    inverse = lax.rsqrt(variance + EPSILON)
    return centred * inverse, inverse


def norm_back(grad_out, normed, inverse, gain_row):
    scaled = grad_out * gain_row
    inner = (
        scaled
        - jnp.mean(scaled, axis=-1, keepdims=True)
        - normed * jnp.mean(scaled * normed, axis=-1, keepdims=True)
    )
    return inner * inverse


def dot(left, right):
    return jnp.dot(left, right, preferred_element_type=f32)


def dot_t(left, right):
    return lax.dot_general(left, right, (((1,), (1,)), ((), ())), preferred_element_type=f32)


def t_dot(left, right):
    return lax.dot_general(left, right, (((0,), (0,)), ((), ())), preferred_element_type=f32)


TB = 32
MASKED = -1e30


def first_position(block):
    return block % NX * 2 + block // NX


def attention_setup(slope_ref, bias_ref, pos_ref, head):
    blocks, rows, lanes = pos_ref.shape
    slope = slope_ref[head]
    steps = lax.broadcasted_iota(jnp.int32, (rows, lanes), 0).astype(f32) * 8.0
    for block in range(blocks):
        at = steps + float(first_position(block))
        pos_ref[block] = at
        bias_ref[block] = at * slope
    return slope


def query_positions(start):
    lane = lax.broadcasted_iota(jnp.int32, (1, 8 * TB), 1)
    block, step = lane // TB, lane % TB
    return ((start + step) * 8 + first_position(block)).astype(f32)


def masked_scores(keys, queries, bias_ref, pos_ref, slope, i):
    count = 8 * TB * (i + 1)
    raw = lax.dot_general(
        keys, queries, (((1,), (1,)), ((), ())), preferred_element_type=f32
    )
    offset = slope * float(8 * TB * i)
    half = bias_ref.shape[2]
    bias = bias_ref[:, : TB * (i + 1), :].reshape(count, half) - offset
    pos = pos_ref[:, : TB * (i + 1), :].reshape(count, half)
    at = query_positions(TB * i)
    parts = [
        jnp.where(
            pos <= at[:, side * half : (side + 1) * half],
            raw[:, side * half : (side + 1) * half] + bias,
            MASKED,
        )
        for side in range(2)
    ]
    return jnp.concatenate(parts, 1)


def block_rows(ref, start, stop):
    return ref[:, start:stop, :].reshape(8 * (stop - start), ref.shape[2])


def attention_kernel(slope_ref, q_ref, k_ref, v_ref, ctx_ref, lse_ref, bias_ref, pos_ref):
    pair, side = pl.program_id(0), pl.program_id(1)
    slope = attention_setup(slope_ref, bias_ref, pos_ref, pair * 2 + side)
    lanes = lax.broadcasted_iota(jnp.int32, (1, 2 * HEAD_DIM), 1) // HEAD_DIM
    mine = lanes == side
    pick = mine.astype(bf16)
    for i in range(q_ref.shape[1] // TB):
        queries = block_rows(q_ref, TB * i, TB * (i + 1)) * (pick * (HEAD_DIM**-0.5))
        keys = block_rows(k_ref, 0, TB * (i + 1))
        values = block_rows(v_ref, 0, TB * (i + 1))
        s = masked_scores(keys, queries, bias_ref, pos_ref, slope, i)
        top = jnp.max(s, axis=0, keepdims=True)
        e = jnp.exp(s - top)
        total = jnp.sum(e, axis=0, keepdims=True)
        att = (e * (1.0 / total)).astype(bf16)
        ctx = lax.dot_general(
            values, att, (((0,), (0,)), ((), ())), preferred_element_type=f32
        ).T.reshape(8, TB, 2 * HEAD_DIM)
        before = ctx_ref[:, TB * i : TB * (i + 1), :]
        ctx_ref[:, TB * i : TB * (i + 1), :] = jnp.where(
            mine[:, None, :], ctx.astype(bf16), before
        )
        lse_ref[0, i : i + 1, :] = top + jnp.log(total)


def attention_back_kernel(
    slope_ref, q_ref, k_ref, v_ref, do_ref, lse_ref, out_ref, bias_ref, pos_ref, dk_ref, dv_ref
):
    pair, side = pl.program_id(0), pl.program_id(1)
    slope = attention_setup(slope_ref, bias_ref, pos_ref, pair * 2 + side)
    lanes = lax.broadcasted_iota(jnp.int32, (1, 2 * HEAD_DIM), 1) // HEAD_DIM
    mine = lanes == side
    pick = mine.astype(bf16)
    scale = HEAD_DIM**-0.5
    width = 2 * HEAD_DIM

    @pl.when(side == 0)
    def _():
        dk_ref[...] = jnp.zeros_like(dk_ref)
        dv_ref[...] = jnp.zeros_like(dv_ref)

    at_q = pl.ds(pl.multiple_of(pair * width, width), width)
    for i in range(q_ref.shape[1] // TB):
        queries = block_rows(q_ref, TB * i, TB * (i + 1)) * (pick * scale)
        grads = block_rows(do_ref, TB * i, TB * (i + 1)) * pick
        keys = block_rows(k_ref, 0, TB * (i + 1))
        values = block_rows(v_ref, 0, TB * (i + 1))
        s = masked_scores(keys, queries, bias_ref, pos_ref, slope, i)
        att = jnp.exp(s - lse_ref[0, i : i + 1, :])
        d_prob = lax.dot_general(
            values, grads, (((1,), (1,)), ((), ())), preferred_element_type=f32
        )
        inner = jnp.sum(att * d_prob, axis=0, keepdims=True)
        ds = (att * (d_prob - inner)).astype(bf16)
        shape = (8, TB * (i + 1), width)
        dv_ref[:, : TB * (i + 1), :] += jnp.dot(
            att.astype(bf16), grads, preferred_element_type=f32
        ).reshape(shape)
        dk_ref[:, : TB * (i + 1), :] += jnp.dot(
            ds, queries, preferred_element_type=f32
        ).reshape(shape)
        dq = lax.dot_general(
            keys, ds, (((0,), (0,)), ((), ())), preferred_element_type=f32
        ).T.reshape(8, TB, width)
        before = out_ref[:, TB * i : TB * (i + 1), at_q]
        out_ref[:, TB * i : TB * (i + 1), at_q] = jnp.where(
            mine[:, None, :], (dq * scale).astype(bf16), before
        )

    @pl.when(side == 1)
    def _():
        part = out_ref.shape[2] // 3
        at_k = pl.ds(pl.multiple_of(part + pair * width, width), width)
        at_v = pl.ds(pl.multiple_of(2 * part + pair * width, width), width)
        out_ref[:, :, at_k] = dk_ref[...].astype(bf16)
        out_ref[:, :, at_v] = dv_ref[...].astype(bf16)


def qkv_specs(rows, pairs):
    width = 2 * HEAD_DIM
    return [
        pl.BlockSpec((8, rows, width), lambda g, h, *_, first=first: (0, 0, first + g))
        for first in (0, pairs, 2 * pairs)
    ]


def attention(qkv, slopes):
    rows, part = qkv.shape[1], qkv.shape[2] // 3
    pairs, width = part // (2 * HEAD_DIM), 2 * HEAD_DIM
    return pl.pallas_call(
        attention_kernel,
        grid_spec=pltpu.PrefetchScalarGridSpec(
            num_scalar_prefetch=1,
            grid=(pairs, 2),
            in_specs=qkv_specs(rows, pairs),
            out_specs=[
                pl.BlockSpec((8, rows, width), lambda g, h, *_: (0, 0, g)),
                pl.BlockSpec((1, rows // TB, 8 * TB), lambda g, h, *_: (2 * g + h, 0, 0)),
            ],
            scratch_shapes=[
                pltpu.VMEM((8, rows, width), f32),
                pltpu.VMEM((8, rows, width), f32),
            ],
        ),
        out_shape=[
            jax.ShapeDtypeStruct((8, rows, part), bf16),
            jax.ShapeDtypeStruct((2 * pairs, rows // TB, 8 * TB), f32),
        ],
        compiler_params=pltpu.CompilerParams(vmem_limit_bytes=40 << 20),
        cost_estimate=cost(10.2),
        name="attention",
    )(slopes, qkv, qkv, qkv)


def attention_back(qkv, d_ctx, lse, slopes):
    rows, part = qkv.shape[1], qkv.shape[2] // 3
    pairs, width = part // (2 * HEAD_DIM), 2 * HEAD_DIM
    return pl.pallas_call(
        attention_back_kernel,
        grid_spec=pltpu.PrefetchScalarGridSpec(
            num_scalar_prefetch=1,
            grid=(pairs, 2),
            in_specs=qkv_specs(rows, pairs)
            + [
                pl.BlockSpec((8, rows, width), lambda g, h, *_: (0, 0, g)),
                pl.BlockSpec((1, rows // TB, 8 * TB), lambda g, h, *_: (2 * g + h, 0, 0)),
            ],
            out_specs=pl.BlockSpec((8, rows, 3 * part), lambda g, h, *_: (0, 0, 0)),
            scratch_shapes=[pltpu.VMEM((8, rows, width), f32) for _ in range(4)],
        ),
        out_shape=jax.ShapeDtypeStruct((8, rows, 3 * part), bf16),
        compiler_params=pltpu.CompilerParams(vmem_limit_bytes=40 << 20),
        cost_estimate=cost(11.5),
        name="attention_back",
    )(slopes, qkv, qkv, qkv, d_ctx, lse)


def take(values, index, axis, size=1):
    starts = [0] * values.ndim
    starts[axis] = index
    sizes = list(values.shape)
    sizes[axis] = size
    return lax.dynamic_slice(values, starts, sizes)


def put(values, block, index, axis):
    starts = [0] * values.ndim
    starts[axis] = index
    return lax.dynamic_update_slice(values, block, starts)


def pick_kernel(info_ref, weight_ref, *refs, groups):
    outs, sems = refs[-NX - 1 : -1], refs[-1]
    rows, cols = outs[0].shape[0], outs[0].shape[1] // groups
    copies = []
    for k in range(NX):
        for group in range(groups):
            at = group * NX * 2 * cols + info_ref[1 + k] * cols
            copies.append(
                pltpu.make_async_copy(
                    weight_ref.at[
                        pl.ds(pl.multiple_of(info_ref[0] * rows, rows), rows),
                        pl.ds(pl.multiple_of(at, cols), cols),
                    ],
                    outs[k].at[:, pl.ds(group * cols, cols)],
                    sems.at[k * groups + group],
                )
            )
    for copy in copies:
        copy.start()
    for copy in copies:
        copy.wait()


def pick_columns(weight, groups, after):
    ax, az, core = lax.axis_index("x"), lax.axis_index("z"), lax.axis_index("c")
    rows, cols = weight.shape[0] // NZ, weight.shape[1] // (NX * 2)
    info = jnp.stack([az] + [(ax + k) % NX * 2 + core for k in range(NX)]).astype(jnp.int32)
    return pl.pallas_call(
        functools.partial(pick_kernel, groups=groups),
        grid_spec=pltpu.PrefetchScalarGridSpec(
            num_scalar_prefetch=1,
            grid=(1,),
            in_specs=[pl.BlockSpec(memory_space=pl.ANY)] * (1 + len(after)),
            out_specs=[pl.BlockSpec(memory_space=pl.ANY)] * NX,
            scratch_shapes=[pltpu.SemaphoreType.DMA((NX * groups,))],
        ),
        out_shape=[jax.ShapeDtypeStruct((rows, cols), weight.dtype)] * NX,
        compiler_params=kernel_params(),
        cost_estimate=cost(1.6),
        name="pick_columns",
    )(info, weight, *after)


def quarter_of_columns(weight, groups, after=()):
    ax, yh = lax.axis_index("x"), lax.axis_index("yh")
    pieces = pick_columns(weight, groups, after)
    by_x = jnp.zeros((NX,) + pieces[0].shape, bf16)
    for k in range(NX):
        got = pieces[k] if k == 0 else along_x(pieces[k], k)
        by_x = put(by_x, got[None], (ax - k) % NX, 0)
    other = along_y(by_x, 1, 1)
    by_xy = jnp.where(yh == 0, jnp.stack([by_x, other], 1), jnp.stack([other, by_x], 1))
    return by_xy.reshape((8,) + pieces[0].shape)


def assemble_kernel(info_ref, *refs):
    blocks, out_ref = refs[:NZ], refs[NZ]
    for k in range(NZ):
        out_ref[0, info_ref[k]] = blocks[k][0]


def assemble_planes(blocks):
    az = lax.axis_index("z")
    _, rows, cols = blocks[0].shape
    info = jnp.stack([(az - k) % NZ for k in range(NZ)]).astype(jnp.int32)
    full = pl.pallas_call(
        assemble_kernel,
        grid_spec=pltpu.PrefetchScalarGridSpec(
            num_scalar_prefetch=1,
            grid=(8,),
            in_specs=[pl.BlockSpec((1, rows, cols), lambda i, info: (i, 0, 0))] * NZ,
            out_specs=pl.BlockSpec((1, NZ, rows, cols), lambda i, info: (i, 0, 0, 0)),
        ),
        out_shape=jax.ShapeDtypeStruct((8, NZ, rows, cols), blocks[0].dtype),
        compiler_params=kernel_params(),
        cost_estimate=cost(4.0),
        name="assemble",
    )(info, *blocks)
    return full.reshape(8 * NZ * rows, cols)


def copy_kernel(source_ref, *refs):
    refs[-1][...] = source_ref[...]


def copy_after(values, after):
    rows, cols = values.shape
    spec = pl.BlockSpec((rows // 8, cols), lambda i: (i, 0))
    return pl.pallas_call(
        copy_kernel,
        grid=(8,),
        in_specs=[spec] + [pl.BlockSpec(memory_space=pl.ANY)] * len(after),
        out_specs=spec,
        out_shape=jax.ShapeDtypeStruct(values.shape, values.dtype),
        compiler_params=kernel_params(),
        cost_estimate=cost(4.0),
        name="copy_after",
    )(values, *after)


SLOTS = ("z", "yl", "yh")


def sum_kernel(pieces_ref, out_ref):
    out_ref[...] = jnp.sum(pieces_ref[...].astype(f32), axis=0).astype(out_ref.dtype)


def sum_over_slots(pieces, name, after=()):
    got = lax.all_to_all(pieces, SLOTS, 0, 0, tiled=True)
    if after:
        got = gate([got], list(after))[0]
    count, rows, cols = got.shape
    step = min(rows, 32)
    return pl.pallas_call(
        sum_kernel,
        grid=(rows // step,),
        in_specs=[pl.BlockSpec((count, step, cols), lambda i: (0, i, 0))],
        out_specs=pl.BlockSpec((step, cols), lambda i: (i, 0)),
        out_shape=jax.ShapeDtypeStruct((rows, cols), bf16),
        compiler_params=kernel_params(),
        cost_estimate=cost(3.0),
        name=name + "_sum",
    )(got)


def column_pieces(grad):
    part, cols = grad.shape[0] // (2 * NX), grad.shape[1]
    pieces = grad.reshape(NX, 2, 2, NZ, part // (2 * NZ), cols).transpose(3, 2, 1, 0, 4, 5)
    return pieces.reshape(16, NX * (part // (2 * NZ)), cols)


def row_planes(own):
    az, yl, yh, core = (lax.axis_index(n) for n in ("z", "yl", "yh", "c"))
    own = move(own)
    other = along_y(own, 1, 0)
    both = jnp.where(yl == 0, jnp.stack([own, other]), jnp.stack([other, own]))
    full = jnp.zeros((NZ,) + both.shape, both.dtype)
    for k in range(NZ):
        got = both if k == 0 else along_z(both, k)
        full = put(full, got[None], (az - k) % NZ, 0)
    theirs = across_core(full)
    out = jnp.where(core == 0, jnp.stack([full, theirs], 2), jnp.stack([theirs, full], 2))
    return out.reshape((8, 2) + own.shape)


def place_kernel(info_ref, *refs, groups):
    out_ref = refs[-1]
    core, step = info_ref[0], pl.program_id(0)
    for side in range(2):
        for k in range(NZ):
            ref = refs[side * NZ + k]

            @pl.when(step // 2 == k)
            def _(ref=ref, side=side):
                block = ref[step % 2]
                cols = block.shape[-1] // groups
                for group in range(groups):
                    for chip in range(NX):
                        at = (group * 2 * NX + chip * 2 + (core ^ side)) * cols
                        out_ref[:, pl.ds(pl.multiple_of(at, cols), cols)] = block[
                            chip, :, group * cols : (group + 1) * cols
                        ].astype(f32)


def place_planes(pieces, groups):
    az, yl, core = lax.axis_index("z"), lax.axis_index("yl"), lax.axis_index("c")
    _, _, rows, n = pieces[0].shape
    info = jnp.stack([core] + [(yl ^ i) * NZ + (az - k) % NZ for k in range(NZ) for i in range(2)])
    full = pl.BlockSpec(pieces[0].shape, lambda i, info: (0, 0, 0, 0))
    return pl.pallas_call(
        functools.partial(place_kernel, groups=groups),
        grid_spec=pltpu.PrefetchScalarGridSpec(
            num_scalar_prefetch=1,
            grid=(8,),
            in_specs=[full] * 8,
            out_specs=pl.BlockSpec((rows, 8 * n), lambda i, info: (info[1 + i], 0)),
        ),
        out_shape=jax.ShapeDtypeStruct((8 * rows, 8 * n), f32),
        compiler_params=kernel_params(),
        cost_estimate=cost(7.0),
        name="place_planes",
    )(info.astype(jnp.int32), *pieces)


def place_columns(own, groups):
    both = jnp.stack([own, along_y(own, 1, 0)])
    planes = [both] + [along_z(both, k) for k in (1, 2, 3)]
    return place_planes(planes + [across_core(p) for p in planes], groups)


def rows_of_member(sums):
    ax = lax.axis_index("x")
    out = jnp.zeros(sums.shape, sums.dtype)
    for k in range(NX):
        block = take(sums, (ax + k) % NX, 0)
        got = block if k == 0 else along_x(block, k)
        out = put(out, got, (ax - k) % NX, 0)
    return out


def local(tokens, lengths, vectors, fc1_bias, w_qkv, w_dense, w_fc1, w_fc2, cotangent):
    rows, width = tokens.shape
    ax, az = lax.axis_index("x"), lax.axis_index("z")
    core, yh = lax.axis_index("c"), lax.axis_index("yh")
    part = width // 8
    ff_part = fc1_bias.shape[0]
    heads = part // HEAD_DIM
    slot = rows * 8
    own_pos = jnp.arange(rows, dtype=jnp.int32) * 8 + ax * 2 + yh
    valid = (own_pos < lengths[0]).astype(f32)[:, None]

    tok = move(tokens)
    quarter_qkv, tok = gate([quarter_of_columns(w_qkv, 3), tok], [])
    tok_blocks = gather_rows(tok)

    packed = jnp.concatenate([vectors, fc1_bias.reshape(ff_part // part, part)])
    by_x = jnp.zeros((NX,) + packed.shape, f32)
    for k in range(NX):
        got = packed if k == 0 else along_x(packed, k)
        by_x = put(by_x, got[None], (ax - k) % NX, 0)
    other = along_y(by_x, 0, 1)
    packed = jnp.where(yh == 0, jnp.stack([by_x, other], 1), jnp.stack([other, by_x], 1))
    packed = packed.reshape(8, -1, part)
    vec_all = packed[:, :8].transpose(1, 0, 2).reshape(8, width)
    packed_part = take(packed, ax * 2 + core, 0)[0]
    vec_part, bias_part = packed_part[:8], packed_part[8:].reshape(ff_part)

    wq = lax.all_gather(quarter_qkv, "z", axis=1, tiled=True).reshape(width, 3 * part)
    quarter_fc1 = quarter_of_columns(w_fc1, 1, [quarter_qkv])
    wf1 = lax.all_gather(quarter_fc1, "z", axis=1, tiled=True).reshape(width, ff_part)
    wd = move(w_dense)
    rows_of = lambda n: jax.ShapeDtypeStruct((8, rows, n), bf16)
    dm_own = move((valid * cotangent.astype(f32)).astype(bf16))
    (dm,) = row_call(
        collect_kernel, gather_rows(dm_own), [], [], [rows_of(width)], "collect", 5.0
    )

    bias_qkv = jnp.concatenate([vec_part[2], jnp.zeros((part,), f32), vec_part[3]])
    (a_b,) = row_call(norm_kernel, tok_blocks, [vec_all], [], [rows_of(width)], "norm", 8.0)
    a_b, bias_qkv = gate([a_b, bias_qkv[None]], [quarter_fc1, wd, dm])
    qkv = project_qkv(a_b, wq, bias_qkv)

    head = ((ax * 2 + core) * heads + jnp.arange(heads, dtype=jnp.int32)).astype(f32)
    slopes = jnp.exp2(-8.0 * (head + 1.0) / (heads * 8))
    ctx, lse = attention(qkv, slopes)
    attn_terms = scatter_rows(ctx, wd, False, "dense")
    wf2 = move_late(copy_after(w_fc2, [quarter_fc1, vec_all, wd, dm]), [ctx])
    d_act = dot_t(dm.reshape(slot, width), wf2).astype(bf16).reshape(8, rows, ff_part)
    attn_terms = gate(attn_terms, [d_act])
    hidden = tok.astype(f32) + total(attn_terms) + vec_all[4]
    unit_two, inverse_two = normalize(hidden)
    c_own = (unit_two * vec_all[5] + vec_all[6]).astype(bf16)
    c_blocks = gather_rows(c_own)
    c_b, act_b, du_b, du_sum = row_call(
        mlp_kernel,
        c_blocks,
        [wf1, bias_part[None]],
        [d_act],
        [
            rows_of(width),
            rows_of(ff_part),
            rows_of(ff_part),
            jax.ShapeDtypeStruct((1, ff_part), f32),
        ],
        "feed_forward",
        13.7,
    )
    dc_chips = mine_part(
        du_b, wf1, theirs_part(du_b, wf1, True, "fc1_back"), True, "fc1_back"
    )
    dc_terms = send_chips(dc_chips)
    act_late, c_late = gate([act_b, c_b], [dc_chips[0]])
    g_fc2 = t_dot(act_late.reshape(slot, ff_part), dm.reshape(slot, width)).astype(bf16)
    g_fc1 = t_dot(c_late.reshape(slot, width), du_b.reshape(slot, ff_part)).astype(bf16)
    dc_terms = gate(dc_terms, [g_fc2, g_fc1])
    dc = total(dc_terms)
    dh = dm_own.astype(f32) + norm_back(dc, unit_two, inverse_two, vec_all[5])
    dh_own = dh.astype(bf16)
    dh_blocks = gather_rows(dh_own)
    dh_b, dctx = row_call(
        ctx_back_kernel, dh_blocks, [wd], [], [rows_of(width), rows_of(part)], "dense_back", 6.8
    )
    d_proj = attention_back(qkv, dctx, lse, slopes)
    g_qkv = t_dot(a_b.reshape(slot, width), d_proj.reshape(slot, 3 * part)).astype(bf16)
    d_proj_late, g_qkv = gate([d_proj, g_qkv], [])
    da_chips = mine_part(
        d_proj_late, wq, theirs_part(d_proj_late, wq, True, "qkv_back"), True, "qkv_back"
    )
    da_terms = send_chips(da_chips)
    act_late = gate([act_late], [da_chips[0]])[0]
    fc2_terms = scatter_rows(act_late, wf2, False, "fc2")
    g_dense = t_dot(ctx.reshape(slot, part), dh_b.reshape(slot, width)).astype(bf16)
    da = total(da_terms)
    own_unit, own_inverse = normalize(tok.astype(f32))
    d_tokens = move((dh + norm_back(da, own_unit, own_inverse, vec_all[0])).astype(bf16))
    d_proj = d_proj.reshape(slot, 3 * part)

    out_own = (hidden + total(fc2_terms) + vec_all[7]).astype(bf16)
    output = (valid * move(out_own).astype(f32)).astype(bf16)

    home = yh == core
    fc2_sum = sum_over_slots(g_fc2.reshape(16, ff_part // 16, width), "fc2")
    grad_fc2 = row_planes(fc2_sum).reshape(ff_part, width).astype(f32)
    fc1_sum = sum_over_slots(column_pieces(g_fc1), "fc1")
    fc1_sum = fc1_sum.reshape(NX, part // (2 * NZ), ff_part)
    grad_fc1 = place_columns(rows_of_member(fc1_sum), 1)
    qkv_sum = sum_over_slots(column_pieces(g_qkv), "qkv")
    qkv_sum = qkv_sum.reshape(NX, part // (2 * NZ), 3 * part)
    grad_qkv = place_columns(rows_of_member(qkv_sum), 3)

    token_terms = jnp.stack(
        [
            jnp.sum(da * own_unit, 0),
            jnp.sum(da, 0),
            jnp.sum(dh_own.astype(f32), 0),
            jnp.sum(dc * unit_two, 0),
            jnp.sum(dc, 0),
            jnp.sum(dm_own.astype(f32), 0),
        ]
    ).reshape(6, NX, 2, part)
    chip_terms = take(token_terms, core, 2) + across_core(take(token_terms, 1 - core, 2))
    chip_terms = chip_terms.reshape(6, NX, part)
    terms = take(chip_terms, ax, 1)
    for k in (1, 2, 3):
        terms = terms + along_x(take(chip_terms, (ax + k) % NX, 1), k)
    terms = jnp.concatenate(
        [
            terms[:, 0],
            jnp.sum(d_proj[:, :part].astype(f32), 0)[None],
            jnp.sum(d_proj[:, 2 * part :].astype(f32), 0)[None],
            du_sum.reshape(ff_part // part, part),
        ]
    ).astype(bf16)
    each = terms.size // 16
    terms = jnp.pad(terms.reshape(16, 1, each), ((0, 0), (0, 15), (0, width - each)))
    count = part // 16
    summed = sum_over_slots(
        jnp.concatenate([g_dense.reshape(16, count, width), terms], 1), "dense"
    )
    summed = row_planes(summed).reshape(16, count + 16, width).astype(f32)
    grad_dense = summed[:, :count].reshape(part, width)
    terms = summed[:, count, :each].reshape(12, part)
    grad_vectors = jnp.concatenate([terms[:2], terms[6:8], terms[2:6]])
    grad_bias = terms[8:].reshape(ff_part)
    return (output, d_tokens, grad_vectors, grad_bias, grad_qkv, grad_dense, grad_fc1, grad_fc2)


def solution(mesh):
    fine = Mesh(np.asarray(mesh.devices).reshape(4, 2, 2, 4, 2), ALL)
    rows = P(("z", "yl", "c", "x", "yh"), None)
    shard = P(("x", "yh"), None)
    return jax.shard_map(
        local,
        mesh=fine,
        in_specs=(
            rows,
            P(("z", "yl", "c")),
            P(None, ("x", "yh")),
            P(("x", "yh")),
            shard,
            shard,
            shard,
            shard,
            rows,
        ),
        out_specs=(
            rows,
            rows,
            P(None, ("x", "yh")),
            P(("x", "yh")),
            shard,
            shard,
            shard,
            shard,
        ),
        check_vma=False,
    )
```

time: 880 us -> 693 us (0.79)
  Pallas kernels: 0 us -> 148 us
  blocking collectives: 133 us -> 0 us
  waiting for transfers between devices: 298 us -> 169 us
  starting transfers between devices: 144 us -> 237 us
  matrix products: 102 us -> 30.9 us
  local copies, waits for them, and re-layouts: 93.7 us -> 39.8 us
  other arithmetic: 78.7 us -> 41.8 us
    pallas_call x0 -> x30, Pallas kernels: none -> 148 us  [the longest x4 33.4 us: row_call(): pl.pallas_call(kernel, grid_spec=pltpu.PrefetchScalarGridSpec(num_scalar_...]
    psum x1 -> x0, waiting for transfers between devices: 117 us -> none  [summed(): return lax.psum(values.astype(bf16), slots)]
    psum x2 -> x0, blocking collectives: 91.4 us -> none  [the longest x1 63.3 us: local(): token_terms = lax.psum(token_terms.astype(bf16), ALL).astype(f32)]
    ppermute x17 -> x31, starting transfers between devices: 55.9 us -> 122 us  [across_core(): return lax.ppermute(values, 'c', [(0, 1), (1, 0)])]
    dot_general x10 -> x0, matrix products: 58.6 us -> none  [the longest x4 25.4 us: dot(): return jnp.dot(left, right, preferred_element_type=f32)]
    ppermute x6 -> x12, waiting for transfers between devices: 68.7 us -> 26.6 us  [along_z(): return lax.ppermute(values, 'z', [(i, (i + step) % NZ) for i in range(NZ)])]
    all_gather x1 -> x0, blocking collectives: 41.3 us -> none  [local(): vec_all = lax.all_gather(vectors, ('x', 'yh'), axis=1, tiled=True)]
    convert_element_type x18 -> x1, local copies, waits for them, and re-layouts: 35.9 us -> 0.09 us  [local(): terms = jnp.concatenate([terms[:, 0], jnp.sum(d_proj[:, :part].astype(f32...]
  transfers between devices with their start and end apart: 66 -> 106, of which waited for: 22 -> 31; matrix products, arithmetic and copies ran while one was open for 23% -> 13% of each run, Pallas kernels for 0% -> 18%
where the time goes in v2:
time: 693 us; the launch traced here: 682 us
  starting transfers between devices  237 us (34%)
  waiting for transfers between devices  169 us (24%)
  Pallas kernels  148 us (21%)
  other arithmetic  41.8 us (6%)
  local copies, waits for them, and re-layouts  39.8 us (6%)
  matrix products  30.9 us (4%)
  between operations  16 us (2%)
    ppermute x31, starting transfers between devices, across_core(): return lax.ppermute(values, 'c', [(0, 1), (1, 0)])  122 us
    ppermute x42, waiting for transfers between devices, along_x(): return lax.ppermute(values, 'x', [(i, (i + step) % NX) for i in range(NX)])  94.3 us
    ppermute x42, starting transfers between devices, along_x(): return lax.ppermute(values, 'x', [(i, (i + step) % NX) for i in range(NX)])  43 us
    all_to_all x4, starting transfers between devices, sum_over_slots(): got = lax.all_to_all(pieces, SLOTS, 0, 0, tiled=True)  34.1 us
    pallas_call x4, Pallas kernels, row_call(): pl.pallas_call(kernel, grid_spec=pltpu.PrefetchScalarGridSpec(num_scalar_...  33.4 us
    ppermute x12, waiting for transfers between devices, along_z(): return lax.ppermute(values, 'z', [(i, (i + step) % NZ) for i in range(NZ)])  26.6 us
    pallas_call x4, Pallas kernels, mine_part(): pl.pallas_call(functools.partial(mine_kernel, contract=contract), grid_sp...  26.5 us
    pallas_call x4, Pallas kernels, theirs_part(): pl.pallas_call(functools.partial(theirs_kernel, contract=contract), grid_...  24.5 us
  transfers between devices with their start and end apart: 106, of which 31 were waited for; matrix products, arithmetic and copies ran while one was open for 13% of the time, Pallas kernels for 18%

profile of v2, /device:TPU:63, one launch (start us, length us, event | category | flops | bytes accessed | tf_op | source)
XLA Modules:
  0.0 682.4 jit_solution(6508224941009136880)
XLA Ops:
  17.6 14.9 %collective-permute-done.3 = bf16[4,64,768]{2,1,0:T(8,128)(2,1)S(1)} collective-permute-done((bf16[4,64,768]{2,1,0:T(8,128)(2,1)S(1)}, bf16[4,64,768]{2,1,0:T(8,128)(2,1)S(1)}, u32[]{:S(2)}, u32[]{:S(2)}) %collective-permute-start.3) | collective-permute-done | bytes 393248 | tf_op jit(solution)/shard_map/ppermute | solution.py:46
  55.4 21.5 %collective-permute-done.16 = bf16[64,1024]{1,0:T(8,128)(2,1)S(1)} collective-permute-done((bf16[64,1024]{1,0:T(8,128)(2,1)S(1)}, bf16[64,1024]{1,0:T(8,128)(2,1)S(1)}, u32[]{:S(2)}, u32[]{:S(2)}) %collective-permute-start.16) | collective-permute-done | bytes 131104 | tf_op jit(solution)/shard_map/ppermute | solution.py:37
  98.0 14.8 %collective-permute-start.22 = (bf16[128,2048]{1,0:T(8,128)(2,1)S(1)}, bf16[128,2048]{1,0:T(8,128)(2,1)S(1)}, u32[]{:S(2)}, u32[]{:S(2)}) collective-permute-start(bf16[128,2048]{1,0:T(8,128)(2,1)S(1)} %get-tuple-element.131.refs_0_), channel_id=1, source_target_pairs={{0,8},{8,0},{1,9},{9,1},{2,10},{10,2},{3,11},{11,3},{4,12},{12,4},... | collective-permute-start | bytes 1572872 | tf_op jit(solution)/shard_map/ppermute | solution.py:33
  119.3 7.7 %collective-permute-done.10.refs_6_ = bf16[128,2048]{1,0:T(8,128)(2,1)} collective-permute-done((bf16[128,2048]{1,0:T(8,128)(2,1)S(1)}, bf16[128,2048]{1,0:T(8,128)(2,1)}, u32[]{:S(2)}, u32[]{:S(2)}) %collective-permute-start.10) | collective-permute-done | bytes 524320 | tf_op jit(solution)/shard_map/ppermute | solution.py:37
  147.0 7.9 %norm.1.refs_0_ = bf16[8,128,2048]{2,1,0:T(8,128)(2,1)} custom-call(s32[8]{0:T(128)} %stack.353.at_ref, bf16[128,2048]{1,0:T(8,128)(2,1)} %get-tuple-element.60.refs_0_, bf16[128,2048]{1,0:T(8,128)(2,1)} %copy-done.42, bf16[128,2048]{1,0:T(8,128)(2,1)} %collective-permute-done.6.refs_2_, bf16[128,2048]{1,0:T(8,128)(2,1)} %copy-done.43, ...), custom_call_target="tpu_custom_call" | custom-call | flops 8000000000 | bytes 25600000 | tf_op jit(solution)/shard_map/norm/pallas_call | solution.py:186
  154.9 7.9 %qkv.1.q_ref.k_ref.v_ref = bf16[8,128,768]{2,1,0:T(8,128)(2,1)} custom-call(bf16[8,128,2048]{2,1,0:T(8,128)(2,1)} %get-tuple-element.66.a_ref, bf16[2048,768]{1,0:T(8,128)(2,1)} %bitcast.247, f32[1,768]{1,0:T(1,128)} %get-tuple-element.67.bias_ref), custom_call_target="tpu_custom_call" | custom-call | flops 7000000000 | bytes 22400000 | tf_op jit(solution)/shard_map/qkv/pallas_call | solution.py:234
  164.2 10.2 %attention.1 = (bf16[8,128,256]{2,1,0:T(8,128)(2,1)S(1)}, f32[4,4,256]{2,1,0:T(4,128)S(1)}) custom-call(f32[4]{0:T(128)S(1)} %multiply_exponential_fusion.slope_ref, bf16[8,128,768]{2,1,0:T(8,128)(2,1)S(1)} %copy-done.3, bf16[8,128,768]{2,1,0:T(8,128)(2,1)S(1)} %copy-done.3, bf16[8,128,768]{2,1,0:T(8,128)(2,1)S(1)} %copy-done.3), custom_call_target="tpu_custom_call" | custom-call | flops 10200000512 | bytes 32640000 | tf_op jit(solution)/shard_map/attention/pallas_call | solution.py:447
  193.1 7.9 %convolution_convert_fusion = bf16[1024,1024]{1,0:T(8,128)(2,1)} fusion(bf16[1024,2048]{1,0:T(8,128)(2,1)} %bitcast.198, bf16[1024,2048]{1,0:T(8,128)(2,1)S(1)} %broadcast_select_fusion.right_ref), kind=kOutput, calls=%fused_computation.14 | convolution fusion | flops 4296015872 | bytes 10485760 | tf_op jit(solution)/shard_map/dot_general | solution.py:301
  211.2 22.9 %collective-permute-start.34 = (bf16[128,2048]{1,0:T(8,128)(2,1)S(1)}, bf16[128,2048]{1,0:T(8,128)(2,1)}, u32[]{:S(2)}, u32[]{:S(2)}) collective-permute-start(bf16[128,2048]{1,0:T(8,128)(2,1)S(1)} %add_convert_fusion.1.refs_0_), channel_id=1, source_target_pairs={{0,8},{8,0},{1,9},{9,1},{2,10},{10,2},{3,11},{11,3},{4,12},{12,4},... | collective-permute-start | bytes 1572872 | tf_op jit(solution)/shard_map/ppermute | solution.py:33
  250.5 13.7 %feed_forward.1 = (bf16[8,128,2048]{2,1,0:T(8,128)(2,1)}, bf16[8,128,1024]{2,1,0:T(8,128)(2,1)}, bf16[8,128,1024]{2,1,0:T(8,128)(2,1)}, f32[1,1024]{1,0:T(1,128)}) custom-call(s32[8]{0:T(128)} %stack.353.at_ref, bf16[128,2048]{1,0:T(8,128)(2,1)} %copy-done.27, bf16[128,2048]{1,0:T(8,128)(2,1)} %collective-permute-done.34.refs_1_, ...), custom_call_target="tpu_custom_call" | custom-call | flops 13699999744 | bytes 43840000 | tf_op jit(solution)/shard_map/feed_forward/pallas_call | solution.py:186
  276.7 7.3 %fc1_back_mine.1 = (f32[128,2048]{1,0:T(8,128)}, bf16[128,2048]{1,0:T(8,128)(2,1)}, bf16[128,2048]{1,0:T(8,128)(2,1)}, bf16[128,2048]{1,0:T(8,128)(2,1)}) custom-call(s32[5]{0:T(128)} %stack.344.info_ref, bf16[8,128,1024]{2,1,0:T(8,128)(2,1)} %get-tuple-element.79.left_ref, bf16[2048,1024]{1,0:T(8,128)(2,1)} %bitcast.246, bf16[512,2048]{1,0:T(8,128)(2,1)} %copy-done.38), custom_call_target="tpu_custom_call" | custom-call | flops 7000000000 | bytes 22400000 | tf_op jit(solution)/shard_map/fc1_back_mine/pallas_call | solution.py:148
  286.9 7.4 %bitcast_convert_fusion.refs_5_ = bf16[2048,1024]{1,0:T(8,128)(2,1)S(1)} fusion(bf16[8,128,2048]{2,1,0:T(8,128)(2,1)} %get-tuple-element.85, bf16[8,128,1024]{2,1,0:T(8,128)(2,1)} %get-tuple-element.79.left_ref), kind=kOutput, calls=%fused_computation | convolution fusion | flops 4297064448 | bytes 10485760 | tf_op jit(solution)/shard_map/dot_general | solution.py:305
  304.8 9.4 %bitcast_convert_fusion.1.refs_4_ = bf16[1024,2048]{1,0:T(8,128)(2,1)} fusion(bf16[8,128,1024]{2,1,0:T(8,128)(2,1)} %get-tuple-element.81.refs_0_, bf16[8,128,2048]{2,1,0:T(8,128)(2,1)} %collect.1.refs_4_.refs_3_), kind=kOutput, calls=%fused_computation.1 | convolution fusion | flops 4297064448 | bytes 10485760 | tf_op jit(solution)/shard_map/dot_general | solution.py:305
  338.6 8.5 %collective-permute-done.50.refs_6_ = bf16[128,2048]{1,0:T(8,128)(2,1)S(1)} collective-permute-done((bf16[128,2048]{1,0:T(8,128)(2,1)S(1)}, bf16[128,2048]{1,0:T(8,128)(2,1)S(1)}, u32[]{:S(2)}, u32[]{:S(2)}) %collective-permute-start.50) | collective-permute-done | bytes 524320 | tf_op jit(solution)/shard_map/ppermute | solution.py:37
  357.7 11.4 %attention_back.1.refs_0_ = bf16[8,128,768]{2,1,0:T(8,128)(2,1)S(1)} custom-call(f32[4]{0:T(128)S(1)} %multiply_exponential_fusion.slope_ref, bf16[8,128,768]{2,1,0:T(8,128)(2,1)S(1)} %copy-done.4, bf16[8,128,768]{2,1,0:T(8,128)(2,1)S(1)} %copy-done.4, bf16[8,128,768]{2,1,0:T(8,128)(2,1)S(1)} %copy-done.4, bf16[8,128,256]{2,1,0:T(8,128)(2,1)S(1)} %copy-done.5, ...), custom_call_target="tpu_custom_call" | custom-call | flops 11500000256 | bytes 36800000 | tf_op jit(solution)/shard_map/attention_back/pallas_call | solution.py:475
  419.9 13.1 %all-to-all-done.3.pieces_ref = bf16[16,64,2048]{2,1,0:T(8,128)(2,1)} async-done(((bf16[16,64,2048]{2,1,0:T(8,128)(2,1)}), bf16[16,64,2048]{2,1,0:T(8,128)(2,1)}, u32[]{:S(2)}, u32[]{:S(2)}) %all-to-all-start.3) | async-done | bytes 4194336 | tf_op jit(solution)/shard_map/all_to_all | solution.py:617
  433.1 10.7 %all-to-all-start.1 = ((bf16[16,128,768]{2,1,0:T(8,128)(2,1)}), bf16[16,128,768]{2,1,0:T(8,128)(2,1)}, u32[]{:S(2)}, u32[]{:S(2)}) async-start(bf16[16,128,768]{2,1,0:T(8,128)(2,1)} %bitcast.188), calls=%async_computation.1 | async-start | bytes 6291456 | tf_op jit(solution)/shard_map/all_to_all | solution.py:617
  459.1 34.6 %collective-permute-start.62 = (f32[6,4,1,256]{3,0,2,1:T(8,128)S(1)}, f32[6,4,1,256]{3,0,2,1:T(8,128)S(1)}, u32[]{:S(2)}, u32[]{:S(2)}) collective-permute-start(f32[6,4,1,256]{3,0,2,1:T(8,128)S(1)} %constant_dynamic-slice_fusion.12), channel_id=1, source_target_pairs={{0,8},{8,0},{1,9},{9,1},{2,10},{10,2},{3,11},{11,3},{4,12},{12,4},... | collective-permute-start | bytes 73736 | tf_op jit(solution)/shard_map/ppermute | solution.py:33
  509.8 9.6 %all-to-all-start = ((bf16[16,32,2048]{2,1,0:T(8,128)(2,1)}), bf16[16,32,2048]{2,1,0:T(8,128)(2,1)}, u32[]{:S(2)}, u32[]{:S(2)}) async-start(bf16[16,32,2048]{2,1,0:T(8,128)(2,1)} %fusion.2), calls=%async_computation | async-start | bytes 4194304 | tf_op jit(solution)/shard_map/all_to_all | solution.py:617
  551.4 13.2 %collective-permute-done.96 = bf16[2,64,2048]{2,1,0:T(8,128)(2,1)S(1)} collective-permute-done((bf16[2,64,2048]{2,1,0:T(8,128)(2,1)S(1)}, bf16[2,64,2048]{2,1,0:T(8,128)(2,1)S(1)}, u32[]{:S(2)}, u32[]{:S(2)}) %collective-permute-start.96) | collective-permute-done | bytes 524320 | tf_op jit(solution)/shard_map/ppermute | solution.py:41
  564.6 10.5 %collective-permute-start.53 = (bf16[512,2048]{1,0:T(8,128)(2,1)}, bf16[512,2048]{1,0:T(8,128)(2,1)}, u32[]{:S(2)}, u32[]{:S(2)}) collective-permute-start(bf16[512,2048]{1,0:T(8,128)(2,1)} %fc2_theirs.1), channel_id=1, source_target_pairs={{0,8},{8,0},{1,9},{9,1},{2,10},{10,2},{3,11},{11,3},{4,12},{12,4},... | collective-permute-start | bytes 6291464 | tf_op jit(solution)/shard_map/ppermute | solution.py:33
  585.8 7.5 %place_planes.3 = f32[256,8192]{1,0:T(8,128)} custom-call(s32[9]{0:T(128)} %stack.389.info_ref, bf16[2,4,32,1024]{3,2,1,0:T(8,128)(2,1)} %copy-done.26, bf16[2,4,32,1024]{3,2,1,0:T(8,128)(2,1)} %collective-permute-done.87.refs_1_, bf16[2,4,32,1024]{3,2,1,0:T(8,128)(2,1)} %collective-permute-done.88.refs_2_, ...), custom_call_target="tpu_custom_call" | custom-call | flops 7000000000 | bytes 22400000 | tf_op jit(solution)/shard_map/place_planes/pallas_call | solution.py:678
  626.4 15.0 %collective-permute-done.55 = bf16[128,2048]{1,0:T(8,128)(2,1)S(1)} collective-permute-done((bf16[128,2048]{1,0:T(8,128)(2,1)}, bf16[128,2048]{1,0:T(8,128)(2,1)S(1)}, u32[]{:S(2)}, u32[]{:S(2)}) %collective-permute-start.55) | collective-permute-done | bytes 524320 | tf_op jit(solution)/shard_map/ppermute | solution.py:37
  649.8 8.1 %collective-permute-done.70 = bf16[2,32,2048]{2,1,0:T(8,128)(2,1)S(1)} collective-permute-done((bf16[2,32,2048]{2,1,0:T(8,128)(2,1)S(1)}, bf16[2,32,2048]{2,1,0:T(8,128)(2,1)S(1)}, u32[]{:S(2)}, u32[]{:S(2)}) %collective-permute-start.70) | collective-permute-done | bytes 262176 | tf_op jit(solution)/shard_map/ppermute | solution.py:41
  (467 shorter events, 370.6 us)
Async XLA Ops:
  7.2 147.7 %all-gather.3.cloned.1.call-start = ((), (), s32[]{:S(2)}) async-start(), calls=%async_computation.4 | async-start | bytes 3932160 | tf_op jit(solution)/shard_map/all_gather | solution.py:736
  34.4 214.8 %all-gather.5.cloned.1.call-start = ((), (), s32[]{:S(2)}) async-start(), calls=%async_computation.5 | async-start | bytes 5242880 | tf_op jit(solution)/shard_map/all_gather | solution.py:738
  36.5 54.3 %collective-permute-start.20 = (bf16[256,2048]{1,0:T(8,128)(2,1)S(1)}, bf16[256,2048]{1,0:T(8,128)(2,1)}, u32[]{:S(2)}, u32[]{:S(2)}) collective-permute-start(bf16[256,2048]{1,0:T(8,128)(2,1)S(1)} %copy-done.23), channel_id=1, source_target_pairs={{1,8},{8,1},{3,10},{10,3},{5,12},{12,5},{7,14},{14,7},{17,24},{24,... | collective-permute-start | bytes 3145736 | tf_op jit(solution)/shard_map/ppermute | solution.py:23
  41.8 47.6 %collective-permute-start.15 = (f32[4,12,256]{2,1,0:T(8,128)S(1)}, f32[4,12,256]{2,1,0:T(8,128)S(1)}, u32[]{:S(2)}, u32[]{:S(2)}) collective-permute-start(f32[4,12,256]{2,1,0:T(8,128)S(1)} %bitcast_dynamic-update-slice_fusion.14), channel_id=1, source_target_pairs={{0,1},{1,0},{16,17},{17,16},{2,3},{3,2},{18,19},{19,18},{4,5},{5,4... | collective-permute-start | bytes 147464 | tf_op jit(solution)/shard_map/ppermute | solution.py:46
  48.8 40.7 %collective-permute-start.6 = (bf16[128,2048]{1,0:T(8,128)(2,1)}, bf16[128,2048]{1,0:T(8,128)(2,1)}, u32[]{:S(2)}, u32[]{:S(2)}) collective-permute-start(bf16[128,2048]{1,0:T(8,128)(2,1)} %get-tuple-element.60.refs_0_), channel_id=1, source_target_pairs={{0,2},{2,4},{4,6},{6,0},{1,3},{3,5},{5,7},{7,1},{8,10},{10,12},{12... | collective-permute-start | bytes 1572872 | tf_op jit(solution)/shard_map/ppermute | solution.py:37
  51.7 38.3 %collective-permute-start.8 = (bf16[128,2048]{1,0:T(8,128)(2,1)}, bf16[128,2048]{1,0:T(8,128)(2,1)}, u32[]{:S(2)}, u32[]{:S(2)}) collective-permute-start(bf16[128,2048]{1,0:T(8,128)(2,1)} %get-tuple-element.60.refs_0_), channel_id=1, source_target_pairs={{0,4},{2,6},{4,0},{6,2},{1,5},{3,7},{5,1},{7,3},{8,12},{10,14},{12... | collective-permute-start | bytes 1572872 | tf_op jit(solution)/shard_map/ppermute | solution.py:37
  90.8 36.2 %collective-permute-start.10 = (bf16[128,2048]{1,0:T(8,128)(2,1)S(1)}, bf16[128,2048]{1,0:T(8,128)(2,1)}, u32[]{:S(2)}, u32[]{:S(2)}) collective-permute-start(bf16[128,2048]{1,0:T(8,128)(2,1)S(1)} %copy-done.6), channel_id=1, source_target_pairs={{0,6},{2,0},{4,2},{6,4},{1,7},{3,1},{5,3},{7,5},{8,14},{10,8},{12,... | collective-permute-start | bytes 1572872 | tf_op jit(solution)/shard_map/ppermute | solution.py:37
  141.5 39.5 %collective-permute-start.33 = (bf16[1024,2048]{1,0:T(8,128)(2,1)}, bf16[1024,2048]{1,0:T(8,128)(2,1)}, u32[]{:S(2)}, u32[]{:S(2)}) collective-permute-start(bf16[1024,2048]{1,0:T(8,128)(2,1)} %copy_after.1), channel_id=1, source_target_pairs={{1,8},{8,1},{3,10},{10,3},{5,12},{12,5},{7,14},{14,7},{17,24},{24,... | collective-permute-start | bytes 12582920 | tf_op jit(solution)/shard_map/ppermute | solution.py:28
  211.2 38.0 %collective-permute-start.34 = (bf16[128,2048]{1,0:T(8,128)(2,1)S(1)}, bf16[128,2048]{1,0:T(8,128)(2,1)}, u32[]{:S(2)}, u32[]{:S(2)}) collective-permute-start(bf16[128,2048]{1,0:T(8,128)(2,1)S(1)} %add_convert_fusion.1.refs_0_), channel_id=1, source_target_pairs={{0,8},{8,0},{1,9},{9,1},{2,10},{10,2},{3,11},{11,3},{4,12},{12,4},... | collective-permute-start | bytes 1572872 | tf_op jit(solution)/shard_map/ppermute | solution.py:33
  297.7 76.6 %all-to-all-start.2 = ((bf16[16,128,1024]{2,1,0:T(8,128)(2,1)}), bf16[16,128,1024]{2,1,0:T(8,128)(2,1)}, u32[]{:S(2)}, u32[]{:S(2)}) async-start(bf16[16,128,1024]{2,1,0:T(8,128)(2,1)} %bitcast.186), calls=%async_computation.2 | async-start | bytes 8388608 | tf_op jit(solution)/shard_map/all_to_all | solution.py:617
  374.2 58.9 %all-to-all-start.3 = ((bf16[16,64,2048]{2,1,0:T(8,128)(2,1)}), bf16[16,64,2048]{2,1,0:T(8,128)(2,1)}, u32[]{:S(2)}, u32[]{:S(2)}) async-start(bf16[16,64,2048]{2,1,0:T(8,128)(2,1)} %bitcast.185), calls=%async_computation.3 | async-start | bytes 8388608 | tf_op jit(solution)/shard_map/all_to_all | solution.py:617
  400.6 55.8 %collective-permute-start.60 = (bf16[128,2048]{1,0:T(8,128)(2,1)}, bf16[128,2048]{1,0:T(8,128)(2,1)S(1)}, u32[]{:S(2)}, u32[]{:S(2)}) collective-permute-start(bf16[128,2048]{1,0:T(8,128)(2,1)} %get-tuple-element.100), channel_id=1, source_target_pairs={{0,2},{2,4},{4,6},{6,0},{1,3},{3,5},{5,7},{7,1},{8,10},{10,12},{12... | collective-permute-start | bytes 1572872 | tf_op jit(solution)/shard_map/ppermute | solution.py:37
  401.7 54.7 %collective-permute-start.59 = (bf16[128,2048]{1,0:T(8,128)(2,1)}, bf16[128,2048]{1,0:T(8,128)(2,1)}, u32[]{:S(2)}, u32[]{:S(2)}) collective-permute-start(bf16[128,2048]{1,0:T(8,128)(2,1)} %get-tuple-element.99), channel_id=1, source_target_pairs={{0,6},{2,0},{4,2},{6,4},{1,7},{3,1},{5,3},{7,5},{8,14},{10,8},{12,... | collective-permute-start | bytes 1572872 | tf_op jit(solution)/shard_map/ppermute | solution.py:37
  402.1 54.3 %collective-permute-start.58 = (bf16[128,2048]{1,0:T(8,128)(2,1)}, bf16[128,2048]{1,0:T(8,128)(2,1)}, u32[]{:S(2)}, u32[]{:S(2)}) collective-permute-start(bf16[128,2048]{1,0:T(8,128)(2,1)} %get-tuple-element.98), channel_id=1, source_target_pairs={{0,4},{2,6},{4,0},{6,2},{1,5},{3,7},{5,1},{7,3},{8,12},{10,14},{12... | collective-permute-start | bytes 1572872 | tf_op jit(solution)/shard_map/ppermute | solution.py:37
  433.1 76.7 %all-to-all-start.1 = ((bf16[16,128,768]{2,1,0:T(8,128)(2,1)}), bf16[16,128,768]{2,1,0:T(8,128)(2,1)}, u32[]{:S(2)}, u32[]{:S(2)}) async-start(bf16[16,128,768]{2,1,0:T(8,128)(2,1)} %bitcast.188), calls=%async_computation.1 | async-start | bytes 6291456 | tf_op jit(solution)/shard_map/all_to_all | solution.py:617
  453.8 49.5 %collective-permute-start.86 = (bf16[4,32,1024]{2,1,0:T(8,128)(2,1)}, bf16[4,32,1024]{2,1,0:T(8,128)(2,1)}, u32[]{:S(2)}, u32[]{:S(2)}) collective-permute-start(bf16[4,32,1024]{2,1,0:T(8,128)(2,1)} %constant_dynamic-update-slice_fusion), channel_id=1, source_target_pairs={{0,16},{1,17},{16,0},{17,1},{2,18},{3,19},{18,2},{19,3},{4,20},{5,... | collective-permute-start | bytes 786440 | tf_op jit(solution)/shard_map/ppermute | solution.py:46
  455.4 53.3 %collective-permute-start.95 = (bf16[64,2048]{1,0:T(8,128)(2,1)S(1)}, bf16[64,2048]{1,0:T(8,128)(2,1)}, u32[]{:S(2)}, u32[]{:S(2)}) collective-permute-start(bf16[64,2048]{1,0:T(8,128)(2,1)S(1)} %broadcast_select_fusion.5), channel_id=1, source_target_pairs={{0,16},{1,17},{16,0},{17,1},{2,18},{3,19},{18,2},{19,3},{4,20},{5,... | collective-permute-start | bytes 786440 | tf_op jit(solution)/shard_map/ppermute | solution.py:46
  459.1 35.4 %collective-permute-start.62 = (f32[6,4,1,256]{3,0,2,1:T(8,128)S(1)}, f32[6,4,1,256]{3,0,2,1:T(8,128)S(1)}, u32[]{:S(2)}, u32[]{:S(2)}) collective-permute-start(f32[6,4,1,256]{3,0,2,1:T(8,128)S(1)} %constant_dynamic-slice_fusion.12), channel_id=1, source_target_pairs={{0,8},{8,0},{1,9},{9,1},{2,10},{10,2},{3,11},{11,3},{4,12},{12,4},... | collective-permute-start | bytes 73736 | tf_op jit(solution)/shard_map/ppermute | solution.py:33
  500.2 38.4 %collective-permute-start.61 = (bf16[128,2048]{1,0:T(8,128)(2,1)S(1)}, bf16[128,2048]{1,0:T(8,128)(2,1)}, u32[]{:S(2)}, u32[]{:S(2)}) collective-permute-start(bf16[128,2048]{1,0:T(8,128)(2,1)S(1)} %fusion.12), channel_id=1, source_target_pairs={{1,8},{8,1},{3,10},{10,3},{5,12},{12,5},{7,14},{14,7},{17,24},{24,... | collective-permute-start | bytes 1572872 | tf_op jit(solution)/shard_map/ppermute | solution.py:23
  504.5 44.0 %collective-permute-start.87 = (bf16[2,4,32,1024]{3,2,1,0:T(8,128)(2,1)S(1)}, bf16[2,4,32,1024]{3,2,1,0:T(8,128)(2,1)}, u32[]{:S(2)}, u32[]{:S(2)}) collective-permute-start(bf16[2,4,32,1024]{3,2,1,0:T(8,128)(2,1)S(1)} %pad_maximum_fusion.1.refs_0_), channel_id=1, source_target_pairs={{0,32},{32,64},{64,96},{96,0},{1,33},{33,65},{65,97},{97,1},{2,34}... | collective-permute-start | bytes 1572872 | tf_op jit(solution)/shard_map/ppermute | solution.py:41
  506.8 69.1 %collective-permute-start.88 = (bf16[2,4,32,1024]{3,2,1,0:T(8,128)(2,1)S(1)}, bf16[2,4,32,1024]{3,2,1,0:T(8,128)(2,1)}, u32[]{:S(2)}, u32[]{:S(2)}) collective-permute-start(bf16[2,4,32,1024]{3,2,1,0:T(8,128)(2,1)S(1)} %pad_maximum_fusion.1.refs_0_), channel_id=1, source_target_pairs={{0,64},{32,96},{64,0},{96,32},{1,65},{33,97},{65,1},{97,33},{2,66}... | collective-permute-start | bytes 1572872 | tf_op jit(solution)/shard_map/ppermute | solution.py:41
  507.9 68.1 %collective-permute-start.89 = (bf16[2,4,32,1024]{3,2,1,0:T(8,128)(2,1)S(1)}, bf16[2,4,32,1024]{3,2,1,0:T(8,128)(2,1)}, u32[]{:S(2)}, u32[]{:S(2)}) collective-permute-start(bf16[2,4,32,1024]{3,2,1,0:T(8,128)(2,1)S(1)} %pad_maximum_fusion.1.refs_0_), channel_id=1, source_target_pairs={{0,96},{32,0},{64,32},{96,64},{1,97},{33,1},{65,33},{97,65},{2,98}... | collective-permute-start | bytes 1572872 | tf_op jit(solution)/shard_map/ppermute | solution.py:41
  509.8 83.4 %all-to-all-start = ((bf16[16,32,2048]{2,1,0:T(8,128)(2,1)}), bf16[16,32,2048]{2,1,0:T(8,128)(2,1)}, u32[]{:S(2)}, u32[]{:S(2)}) async-start(bf16[16,32,2048]{2,1,0:T(8,128)(2,1)} %fusion.2), calls=%async_computation | async-start | bytes 4194304 | tf_op jit(solution)/shard_map/all_to_all | solution.py:617
  603.8 55.7 %collective-permute-start.99 = (bf16[4,2,64,2048]{3,2,1,0:T(8,128)(2,1)}, bf16[4,2,64,2048]{3,2,1,0:T(8,128)(2,1)S(1)}, u32[]{:S(2)}, u32[]{:S(2)}) collective-permute-start(bf16[4,2,64,2048]{3,2,1,0:T(8,128)(2,1)} %bitcast_dynamic-update-slice_fusion), channel_id=1, source_target_pairs={{0,8},{8,0},{1,9},{9,1},{2,10},{10,2},{3,11},{11,3},{4,12},{12,4},... | collective-permute-start | bytes 6291464 | tf_op jit(solution)/shard_map/ppermute | solution.py:33
  (148 other events, 1999.0 us)
Sparse Core Ops, SparseCore 0:
  34.5 42.0 all-gather.2
  145.1 48.4 all-gather.4

commit v3 on v2

--- a/solution.py
+++ b/solution.py
@@ -739,20 +739,19 @@
     wd = move(w_dense)
     rows_of = lambda n: jax.ShapeDtypeStruct((8, rows, n), bf16)
     dm_own = move((valid * cotangent.astype(f32)).astype(bf16))
-    (dm,) = row_call(
-        collect_kernel, gather_rows(dm_own), [], [], [rows_of(width)], "collect", 5.0
-    )
+    dm_own = gate([dm_own], [quarter_qkv])[0]
+    dm = lax.all_gather(dm_own, ("c", "x"), axis=0, tiled=True).reshape(8, rows, width)
 
     bias_qkv = jnp.concatenate([vec_part[2], jnp.zeros((part,), f32), vec_part[3]])
     (a_b,) = row_call(norm_kernel, tok_blocks, [vec_all], [], [rows_of(width)], "norm", 8.0)
-    a_b, bias_qkv = gate([a_b, bias_qkv[None]], [quarter_fc1, wd, dm])
+    a_b, bias_qkv = gate([a_b, bias_qkv[None]], [quarter_fc1, wd])
     qkv = project_qkv(a_b, wq, bias_qkv)
 
     head = ((ax * 2 + core) * heads + jnp.arange(heads, dtype=jnp.int32)).astype(f32)
     slopes = jnp.exp2(-8.0 * (head + 1.0) / (heads * 8))
     ctx, lse = attention(qkv, slopes)
     attn_terms = scatter_rows(ctx, wd, False, "dense")
-    wf2 = move_late(copy_after(w_fc2, [quarter_fc1, vec_all, wd, dm]), [ctx])
+    wf2 = move_late(copy_after(w_fc2, [quarter_fc1, vec_all, wd]), [ctx])
     d_act = dot_t(dm.reshape(slot, width), wf2).astype(bf16).reshape(8, rows, ff_part)
     attn_terms = gate(attn_terms, [d_act])
     hidden = tok.astype(f32) + total(attn_terms) + vec_all[4]

time: 693 us -> 703 us (1.014)
  waiting for transfers between devices: 169 us -> 193 us
    ppermute x7, waiting for transfers between devices: 21.7 us -> 44 us  [along_y(): return lax.ppermute(values, ('yl', 'yh'), pairs)]
    ppermute x31 -> x27, starting transfers between devices: 122 us -> 110 us  [across_core(): return lax.ppermute(values, 'c', [(0, 1), (1, 0)])]
    ppermute x7, starting transfers between devices: 9.07 us -> 20.2 us  [along_y(): return lax.ppermute(values, ('yl', 'yh'), pairs)]
    ppermute x42 -> x39, starting transfers between devices: 43 us -> 37.7 us  [along_x(): return lax.ppermute(values, 'x', [(i, (i + step) % NX) for i in range(NX)])]
    pallas_call x4 -> x3, Pallas kernels: 33.4 us -> 28.2 us  [row_call(): pl.pallas_call(kernel, grid_spec=pltpu.PrefetchScalarGridSpec(num_scalar_...]
    unnamed x137 -> x117, local copies, waits for them, and re-layouts: 16.2 us -> 12.7 us
    ppermute x42 -> x39, waiting for transfers between devices: 94.3 us -> 96.3 us  [along_x(): return lax.ppermute(values, 'x', [(i, (i + step) % NX) for i in range(NX)])]
  transfers between devices with their start and end apart: 106 -> 100, of which waited for: 31 -> 31; matrix products, arithmetic and copies ran while one was open for 13% -> 13% of each run, Pallas kernels for 18% -> 17%
where the time goes in v3:
time: 703 us; the launch traced here: 695 us
  starting transfers between devices  231 us (33%)
  waiting for transfers between devices  193 us (27%)
  Pallas kernels  143 us (20%)
  other arithmetic  44.1 us (6%)
  local copies, waits for them, and re-layouts  36.6 us (5%)
  matrix products  32.3 us (5%)
  between operations  15.8 us (2%)
    ppermute x27, starting transfers between devices, across_core(): return lax.ppermute(values, 'c', [(0, 1), (1, 0)])  110 us
    ppermute x39, waiting for transfers between devices, along_x(): return lax.ppermute(values, 'x', [(i, (i + step) % NX) for i in range(NX)])  96.3 us
    ppermute x7, waiting for transfers between devices, along_y(): return lax.ppermute(values, ('yl', 'yh'), pairs)  44 us
    ppermute x39, starting transfers between devices, along_x(): return lax.ppermute(values, 'x', [(i, (i + step) % NX) for i in range(NX)])  37.7 us
    all_to_all x4, starting transfers between devices, sum_over_slots(): got = lax.all_to_all(pieces, SLOTS, 0, 0, tiled=True)  35.4 us
    pallas_call x3, Pallas kernels, row_call(): pl.pallas_call(kernel, grid_spec=pltpu.PrefetchScalarGridSpec(num_scalar_...  28.2 us
    ppermute x12, waiting for transfers between devices, along_z(): return lax.ppermute(values, 'z', [(i, (i + step) % NZ) for i in range(NZ)])  27 us
    pallas_call x4, Pallas kernels, mine_part(): pl.pallas_call(functools.partial(mine_kernel, contract=contract), grid_sp...  26.6 us
  transfers between devices with their start and end apart: 100, of which 31 were waited for; matrix products, arithmetic and copies ran while one was open for 13% of the time, Pallas kernels for 17%

profile of v3, /device:TPU:63, one launch (start us, length us, event | category | flops | bytes accessed | tf_op | source)
XLA Modules:
  0.0 694.8 jit_solution(14364295841669600938)
XLA Ops:
  17.6 14.9 %collective-permute-done.3 = bf16[4,64,768]{2,1,0:T(8,128)(2,1)S(1)} collective-permute-done((bf16[4,64,768]{2,1,0:T(8,128)(2,1)S(1)}, bf16[4,64,768]{2,1,0:T(8,128)(2,1)S(1)}, u32[]{:S(2)}, u32[]{:S(2)}) %collective-permute-start.3) | collective-permute-done | bytes 393248 | tf_op jit(solution)/shard_map/ppermute | solution.py:46
  43.1 15.8 %collective-permute-start.15 = (f32[4,12,256]{2,1,0:T(8,128)S(1)}, f32[4,12,256]{2,1,0:T(8,128)S(1)}, u32[]{:S(2)}, u32[]{:S(2)}) collective-permute-start(f32[4,12,256]{2,1,0:T(8,128)S(1)} %bitcast_dynamic-update-slice_fusion.14), channel_id=1, source_target_pairs={{0,1},{1,0},{16,17},{17,16},{2,3},{3,2},{18,19},{19,18},{4,5},{5,4... | collective-permute-start | bytes 147464 | tf_op jit(solution)/shard_map/ppermute | solution.py:46
  60.1 12.0 %collective-permute-done.15 = f32[4,12,256]{2,1,0:T(8,128)S(1)} collective-permute-done((f32[4,12,256]{2,1,0:T(8,128)S(1)}, f32[4,12,256]{2,1,0:T(8,128)S(1)}, u32[]{:S(2)}, u32[]{:S(2)}) %collective-permute-start.15) | collective-permute-done | bytes 49184 | tf_op jit(solution)/shard_map/ppermute | solution.py:46
  83.0 39.9 %collective-permute-done.17 = bf16[64,1024]{1,0:T(8,128)(2,1)S(1)} collective-permute-done((bf16[64,1024]{1,0:T(8,128)(2,1)S(1)}, bf16[64,1024]{1,0:T(8,128)(2,1)S(1)}, u32[]{:S(2)}, u32[]{:S(2)}) %collective-permute-start.17) | collective-permute-done | bytes 131104 | tf_op jit(solution)/shard_map/ppermute | solution.py:37
  132.2 10.0 %collective-permute-done.19 = bf16[4,64,1024]{2,1,0:T(8,128)(2,1)S(1)} collective-permute-done((bf16[4,64,1024]{2,1,0:T(8,128)(2,1)S(1)}, bf16[4,64,1024]{2,1,0:T(8,128)(2,1)S(1)}, u32[]{:S(2)}, u32[]{:S(2)}) %collective-permute-start.19) | collective-permute-done | bytes 524320 | tf_op jit(solution)/shard_map/ppermute | solution.py:46
  153.5 7.9 %norm.1.refs_0_ = bf16[8,128,2048]{2,1,0:T(8,128)(2,1)} custom-call(s32[8]{0:T(128)} %stack.344.at_ref, bf16[128,2048]{1,0:T(8,128)(2,1)} %get-tuple-element.60.refs_0_, bf16[128,2048]{1,0:T(8,128)(2,1)} %collective-permute-done.5.refs_1_, bf16[128,2048]{1,0:T(8,128)(2,1)} %copy-done.37, bf16[128,2048]{1,0:T(8,128)(2,1)} %collective-permute-done.7.refs_3_, ...), custom_call_target="tpu_custom_call" | custom-call | flops 8000000000 | bytes 25600000 | tf_op jit(solution)/shard_map/norm/pallas_call | solution.py:186
  161.4 7.5 %qkv.1.q_ref.k_ref.v_ref = bf16[8,128,768]{2,1,0:T(8,128)(2,1)} custom-call(bf16[8,128,2048]{2,1,0:T(8,128)(2,1)} %get-tuple-element.66.a_ref, bf16[2048,768]{1,0:T(8,128)(2,1)} %bitcast.245, f32[1,768]{1,0:T(1,128)} %get-tuple-element.67.bias_ref), custom_call_target="tpu_custom_call" | custom-call | flops 7000000000 | bytes 22400000 | tf_op jit(solution)/shard_map/qkv/pallas_call | solution.py:234
  170.5 10.2 %attention.1 = (bf16[8,128,256]{2,1,0:T(8,128)(2,1)S(1)}, f32[4,4,256]{2,1,0:T(4,128)S(1)}) custom-call(f32[4]{0:T(128)S(1)} %multiply_exponential_fusion.slope_ref, bf16[8,128,768]{2,1,0:T(8,128)(2,1)S(1)} %copy-done.3, bf16[8,128,768]{2,1,0:T(8,128)(2,1)S(1)} %copy-done.3, bf16[8,128,768]{2,1,0:T(8,128)(2,1)S(1)} %copy-done.3), custom_call_target="tpu_custom_call" | custom-call | flops 10200000512 | bytes 32640000 | tf_op jit(solution)/shard_map/attention/pallas_call | solution.py:447
  203.1 9.3 %convolution_convert_fusion.1 = bf16[1024,1024]{1,0:T(8,128)(2,1)} fusion(bf16[1024,2048]{1,0:T(8,128)(2,1)} %all-gather.6.cloned.1.call-done, bf16[1024,2048]{1,0:T(8,128)(2,1)} %broadcast_select_fusion.right_ref), kind=kOutput, calls=%fused_computation.14 | convolution fusion | flops 4296015872 | bytes 10485760 | tf_op jit(solution)/shard_map/dot_general | solution.py:301
  220.6 24.9 %collective-permute-start.27 = (bf16[128,2048]{1,0:T(8,128)(2,1)S(1)}, bf16[128,2048]{1,0:T(8,128)(2,1)}, u32[]{:S(2)}, u32[]{:S(2)}) collective-permute-start(bf16[128,2048]{1,0:T(8,128)(2,1)S(1)} %add_convert_fusion.1.refs_0_), channel_id=1, source_target_pairs={{0,8},{8,0},{1,9},{9,1},{2,10},{10,2},{3,11},{11,3},{4,12},{12,4},... | collective-permute-start | bytes 1572872 | tf_op jit(solution)/shard_map/ppermute | solution.py:33
  262.2 13.7 %feed_forward.1 = (bf16[8,128,2048]{2,1,0:T(8,128)(2,1)}, bf16[8,128,1024]{2,1,0:T(8,128)(2,1)}, bf16[8,128,1024]{2,1,0:T(8,128)(2,1)}, f32[1,1024]{1,0:T(1,128)}) custom-call(s32[8]{0:T(128)} %stack.344.at_ref, bf16[128,2048]{1,0:T(8,128)(2,1)} %copy-done.26, bf16[128,2048]{1,0:T(8,128)(2,1)} %collective-permute-done.27.refs_1_, ...), custom_call_target="tpu_custom_call" | custom-call | flops 13699999744 | bytes 43840000 | tf_op jit(solution)/shard_map/feed_forward/pallas_call | solution.py:186
  309.4 8.5 %all-to-all-start.2 = ((bf16[16,128,1024]{2,1,0:T(8,128)(2,1)}), bf16[16,128,1024]{2,1,0:T(8,128)(2,1)}, u32[]{:S(2)}, u32[]{:S(2)}) async-start(bf16[16,128,1024]{2,1,0:T(8,128)(2,1)} %bitcast.184), calls=%async_computation.2 | async-start | bytes 8388608 | tf_op jit(solution)/shard_map/all_to_all | solution.py:617
  317.9 9.4 %convolution_convert_fusion.refs_4_ = bf16[1024,2048]{1,0:T(8,128)(2,1)} fusion(bf16[1024,1024]{1,0:T(8,128)(2,1)} %bitcast.194, bf16[1024,2048]{1,0:T(8,128)(2,1)} %all-gather.6.cloned.1.call-done), kind=kOutput, calls=%fused_computation.8 | convolution fusion | flops 4297064448 | bytes 10485760 | tf_op jit(solution)/shard_map/dot_general | solution.py:305
  351.9 8.5 %collective-permute-done.43.refs_6_ = bf16[128,2048]{1,0:T(8,128)(2,1)S(1)} collective-permute-done((bf16[128,2048]{1,0:T(8,128)(2,1)S(1)}, bf16[128,2048]{1,0:T(8,128)(2,1)S(1)}, u32[]{:S(2)}, u32[]{:S(2)}) %collective-permute-start.43) | collective-permute-done | bytes 524320 | tf_op jit(solution)/shard_map/ppermute | solution.py:37
  370.9 11.4 %attention_back.1.refs_0_ = bf16[8,128,768]{2,1,0:T(8,128)(2,1)S(1)} custom-call(f32[4]{0:T(128)S(1)} %multiply_exponential_fusion.slope_ref, bf16[8,128,768]{2,1,0:T(8,128)(2,1)S(1)} %copy-done.4, bf16[8,128,768]{2,1,0:T(8,128)(2,1)S(1)} %copy-done.4, bf16[8,128,768]{2,1,0:T(8,128)(2,1)S(1)} %copy-done.4, bf16[8,128,256]{2,1,0:T(8,128)(2,1)S(1)} %copy-done.5, ...), custom_call_target="tpu_custom_call" | custom-call | flops 11500000256 | bytes 36800000 | tf_op jit(solution)/shard_map/attention_back/pallas_call | solution.py:475
  433.2 13.1 %all-to-all-done.3.pieces_ref = bf16[16,64,2048]{2,1,0:T(8,128)(2,1)} async-done(((bf16[16,64,2048]{2,1,0:T(8,128)(2,1)}), bf16[16,64,2048]{2,1,0:T(8,128)(2,1)}, u32[]{:S(2)}, u32[]{:S(2)}) %all-to-all-start.3) | async-done | bytes 4194336 | tf_op jit(solution)/shard_map/all_to_all | solution.py:617
  446.3 10.7 %all-to-all-start.1 = ((bf16[16,128,768]{2,1,0:T(8,128)(2,1)}), bf16[16,128,768]{2,1,0:T(8,128)(2,1)}, u32[]{:S(2)}, u32[]{:S(2)}) async-start(bf16[16,128,768]{2,1,0:T(8,128)(2,1)} %bitcast.186), calls=%async_computation.1 | async-start | bytes 6291456 | tf_op jit(solution)/shard_map/all_to_all | solution.py:617
  472.2 34.7 %collective-permute-start.55 = (f32[6,4,1,256]{3,0,2,1:T(8,128)S(1)}, f32[6,4,1,256]{3,0,2,1:T(8,128)S(1)}, u32[]{:S(2)}, u32[]{:S(2)}) collective-permute-start(f32[6,4,1,256]{3,0,2,1:T(8,128)S(1)} %constant_dynamic-slice_fusion.12), channel_id=1, source_target_pairs={{0,8},{8,0},{1,9},{9,1},{2,10},{10,2},{3,11},{11,3},{4,12},{12,4},... | collective-permute-start | bytes 73736 | tf_op jit(solution)/shard_map/ppermute | solution.py:33
  523.0 9.6 %all-to-all-start = ((bf16[16,32,2048]{2,1,0:T(8,128)(2,1)}), bf16[16,32,2048]{2,1,0:T(8,128)(2,1)}, u32[]{:S(2)}, u32[]{:S(2)}) async-start(bf16[16,32,2048]{2,1,0:T(8,128)(2,1)} %fusion.2), calls=%async_computation | async-start | bytes 4194304 | tf_op jit(solution)/shard_map/all_to_all | solution.py:617
  564.6 13.2 %collective-permute-done.89 = bf16[2,64,2048]{2,1,0:T(8,128)(2,1)S(1)} collective-permute-done((bf16[2,64,2048]{2,1,0:T(8,128)(2,1)S(1)}, bf16[2,64,2048]{2,1,0:T(8,128)(2,1)S(1)}, u32[]{:S(2)}, u32[]{:S(2)}) %collective-permute-start.89) | collective-permute-done | bytes 524320 | tf_op jit(solution)/shard_map/ppermute | solution.py:41
  577.9 10.5 %collective-permute-start.46 = (bf16[512,2048]{1,0:T(8,128)(2,1)}, bf16[512,2048]{1,0:T(8,128)(2,1)}, u32[]{:S(2)}, u32[]{:S(2)}) collective-permute-start(bf16[512,2048]{1,0:T(8,128)(2,1)} %fc2_theirs.1), channel_id=1, source_target_pairs={{0,8},{8,0},{1,9},{9,1},{2,10},{10,2},{3,11},{11,3},{4,12},{12,4},... | collective-permute-start | bytes 6291464 | tf_op jit(solution)/shard_map/ppermute | solution.py:33
  599.0 7.5 %place_planes.3 = f32[256,8192]{1,0:T(8,128)} custom-call(s32[9]{0:T(128)} %stack.380.info_ref, bf16[2,4,32,1024]{3,2,1,0:T(8,128)(2,1)} %copy-done.25, bf16[2,4,32,1024]{3,2,1,0:T(8,128)(2,1)} %collective-permute-done.80.refs_1_, bf16[2,4,32,1024]{3,2,1,0:T(8,128)(2,1)} %collective-permute-done.81.refs_2_, ...), custom_call_target="tpu_custom_call" | custom-call | flops 7000000000 | bytes 22400000 | tf_op jit(solution)/shard_map/place_planes/pallas_call | solution.py:678
  638.8 15.3 %collective-permute-done.48 = bf16[128,2048]{1,0:T(8,128)(2,1)S(1)} collective-permute-done((bf16[128,2048]{1,0:T(8,128)(2,1)}, bf16[128,2048]{1,0:T(8,128)(2,1)S(1)}, u32[]{:S(2)}, u32[]{:S(2)}) %collective-permute-start.48) | collective-permute-done | bytes 524320 | tf_op jit(solution)/shard_map/ppermute | solution.py:37
  662.5 8.1 %collective-permute-done.63 = bf16[2,32,2048]{2,1,0:T(8,128)(2,1)S(1)} collective-permute-done((bf16[2,32,2048]{2,1,0:T(8,128)(2,1)S(1)}, bf16[2,32,2048]{2,1,0:T(8,128)(2,1)S(1)}, u32[]{:S(2)}, u32[]{:S(2)}) %collective-permute-start.63) | collective-permute-done | bytes 262176 | tf_op jit(solution)/shard_map/ppermute | solution.py:41
  (436 shorter events, 352.3 us)
Async XLA Ops:
  7.2 154.2 %all-gather.4.cloned.1.call-start = ((), (), s32[]{:S(2)}) async-start(), calls=%async_computation.4 | async-start | bytes 3932160 | tf_op jit(solution)/shard_map/all_gather | solution.py:736
  34.3 168.8 %all-gather.6.cloned.1.call-start = ((), (), s32[]{:S(2)}) async-start(), calls=%async_computation.5 | async-start | bytes 4718592 | tf_op jit(solution)/shard_map/all_gather | solution.py:743
  37.1 223.8 %all-gather.8.cloned.1.call-start = ((), (), s32[]{:S(2)}) async-start(), calls=%async_computation.6 | async-start | bytes 5242880 | tf_op jit(solution)/shard_map/all_gather | solution.py:738
  39.3 91.5 %collective-permute-start.20 = (bf16[256,2048]{1,0:T(8,128)(2,1)S(1)}, bf16[256,2048]{1,0:T(8,128)(2,1)}, u32[]{:S(2)}, u32[]{:S(2)}) collective-permute-start(bf16[256,2048]{1,0:T(8,128)(2,1)S(1)} %copy-done.22), channel_id=1, source_target_pairs={{1,8},{8,1},{3,10},{10,3},{5,12},{12,5},{7,14},{14,7},{17,24},{24,... | collective-permute-start | bytes 3145736 | tf_op jit(solution)/shard_map/ppermute | solution.py:23
  77.6 50.3 %collective-permute-start.6 = (bf16[128,2048]{1,0:T(8,128)(2,1)S(1)}, bf16[128,2048]{1,0:T(8,128)(2,1)S(1)}, u32[]{:S(2)}, u32[]{:S(2)}) collective-permute-start(bf16[128,2048]{1,0:T(8,128)(2,1)S(1)} %copy-done.6), channel_id=1, source_target_pairs={{0,2},{2,4},{4,6},{6,0},{1,3},{3,5},{5,7},{7,1},{8,10},{10,12},{12... | collective-permute-start | bytes 1572872 | tf_op jit(solution)/shard_map/ppermute | solution.py:37
  78.3 52.0 %collective-permute-start.8 = (bf16[128,2048]{1,0:T(8,128)(2,1)S(1)}, bf16[128,2048]{1,0:T(8,128)(2,1)}, u32[]{:S(2)}, u32[]{:S(2)}) collective-permute-start(bf16[128,2048]{1,0:T(8,128)(2,1)S(1)} %copy-done.6), channel_id=1, source_target_pairs={{0,4},{2,6},{4,0},{6,2},{1,5},{3,7},{5,1},{7,3},{8,12},{10,14},{12... | collective-permute-start | bytes 1572872 | tf_op jit(solution)/shard_map/ppermute | solution.py:37
  78.3 52.2 %collective-permute-start.10 = (bf16[128,2048]{1,0:T(8,128)(2,1)S(1)}, bf16[128,2048]{1,0:T(8,128)(2,1)}, u32[]{:S(2)}, u32[]{:S(2)}) collective-permute-start(bf16[128,2048]{1,0:T(8,128)(2,1)S(1)} %copy-done.6), channel_id=1, source_target_pairs={{0,6},{2,0},{4,2},{6,4},{1,7},{3,1},{5,3},{7,5},{8,14},{10,8},{12,... | collective-permute-start | bytes 1572872 | tf_op jit(solution)/shard_map/ppermute | solution.py:37
  80.2 42.7 %collective-permute-start.17 = (bf16[64,1024]{1,0:T(8,128)(2,1)S(1)}, bf16[64,1024]{1,0:T(8,128)(2,1)S(1)}, u32[]{:S(2)}, u32[]{:S(2)}) collective-permute-start(bf16[64,1024]{1,0:T(8,128)(2,1)S(1)} %get-tuple-element.117), channel_id=1, source_target_pairs={{0,4},{2,6},{4,0},{6,2},{1,5},{3,7},{5,1},{7,3},{8,12},{10,14},{12... | collective-permute-start | bytes 393224 | tf_op jit(solution)/shard_map/ppermute | solution.py:37
  149.9 40.1 %collective-permute-start.26 = (bf16[1024,2048]{1,0:T(8,128)(2,1)}, bf16[1024,2048]{1,0:T(8,128)(2,1)}, u32[]{:S(2)}, u32[]{:S(2)}) collective-permute-start(bf16[1024,2048]{1,0:T(8,128)(2,1)} %copy_after.1), channel_id=1, source_target_pairs={{1,8},{8,1},{3,10},{10,3},{5,12},{12,5},{7,14},{14,7},{17,24},{24,... | collective-permute-start | bytes 12582920 | tf_op jit(solution)/shard_map/ppermute | solution.py:28
  220.6 40.4 %collective-permute-start.27 = (bf16[128,2048]{1,0:T(8,128)(2,1)S(1)}, bf16[128,2048]{1,0:T(8,128)(2,1)}, u32[]{:S(2)}, u32[]{:S(2)}) collective-permute-start(bf16[128,2048]{1,0:T(8,128)(2,1)S(1)} %add_convert_fusion.1.refs_0_), channel_id=1, source_target_pairs={{0,8},{8,0},{1,9},{9,1},{2,10},{10,2},{3,11},{11,3},{4,12},{12,4},... | collective-permute-start | bytes 1572872 | tf_op jit(solution)/shard_map/ppermute | solution.py:33
  309.4 78.0 %all-to-all-start.2 = ((bf16[16,128,1024]{2,1,0:T(8,128)(2,1)}), bf16[16,128,1024]{2,1,0:T(8,128)(2,1)}, u32[]{:S(2)}, u32[]{:S(2)}) async-start(bf16[16,128,1024]{2,1,0:T(8,128)(2,1)} %bitcast.184), calls=%async_computation.2 | async-start | bytes 8388608 | tf_op jit(solution)/shard_map/all_to_all | solution.py:617
  387.5 58.9 %all-to-all-start.3 = ((bf16[16,64,2048]{2,1,0:T(8,128)(2,1)}), bf16[16,64,2048]{2,1,0:T(8,128)(2,1)}, u32[]{:S(2)}, u32[]{:S(2)}) async-start(bf16[16,64,2048]{2,1,0:T(8,128)(2,1)} %bitcast.183), calls=%async_computation.3 | async-start | bytes 8388608 | tf_op jit(solution)/shard_map/all_to_all | solution.py:617
  413.8 55.7 %collective-permute-start.53 = (bf16[128,2048]{1,0:T(8,128)(2,1)}, bf16[128,2048]{1,0:T(8,128)(2,1)S(1)}, u32[]{:S(2)}, u32[]{:S(2)}) collective-permute-start(bf16[128,2048]{1,0:T(8,128)(2,1)} %get-tuple-element.100), channel_id=1, source_target_pairs={{0,2},{2,4},{4,6},{6,0},{1,3},{3,5},{5,7},{7,1},{8,10},{10,12},{12... | collective-permute-start | bytes 1572872 | tf_op jit(solution)/shard_map/ppermute | solution.py:37
  414.9 54.6 %collective-permute-start.52 = (bf16[128,2048]{1,0:T(8,128)(2,1)}, bf16[128,2048]{1,0:T(8,128)(2,1)}, u32[]{:S(2)}, u32[]{:S(2)}) collective-permute-start(bf16[128,2048]{1,0:T(8,128)(2,1)} %get-tuple-element.99), channel_id=1, source_target_pairs={{0,6},{2,0},{4,2},{6,4},{1,7},{3,1},{5,3},{7,5},{8,14},{10,8},{12,... | collective-permute-start | bytes 1572872 | tf_op jit(solution)/shard_map/ppermute | solution.py:37
  415.3 54.3 %collective-permute-start.51 = (bf16[128,2048]{1,0:T(8,128)(2,1)}, bf16[128,2048]{1,0:T(8,128)(2,1)}, u32[]{:S(2)}, u32[]{:S(2)}) collective-permute-start(bf16[128,2048]{1,0:T(8,128)(2,1)} %get-tuple-element.98), channel_id=1, source_target_pairs={{0,4},{2,6},{4,0},{6,2},{1,5},{3,7},{5,1},{7,3},{8,12},{10,14},{12... | collective-permute-start | bytes 1572872 | tf_op jit(solution)/shard_map/ppermute | solution.py:37
  446.3 76.7 %all-to-all-start.1 = ((bf16[16,128,768]{2,1,0:T(8,128)(2,1)}), bf16[16,128,768]{2,1,0:T(8,128)(2,1)}, u32[]{:S(2)}, u32[]{:S(2)}) async-start(bf16[16,128,768]{2,1,0:T(8,128)(2,1)} %bitcast.186), calls=%async_computation.1 | async-start | bytes 6291456 | tf_op jit(solution)/shard_map/all_to_all | solution.py:617
  467.0 49.7 %collective-permute-start.79 = (bf16[4,32,1024]{2,1,0:T(8,128)(2,1)}, bf16[4,32,1024]{2,1,0:T(8,128)(2,1)}, u32[]{:S(2)}, u32[]{:S(2)}) collective-permute-start(bf16[4,32,1024]{2,1,0:T(8,128)(2,1)} %constant_dynamic-update-slice_fusion), channel_id=1, source_target_pairs={{0,16},{1,17},{16,0},{17,1},{2,18},{3,19},{18,2},{19,3},{4,20},{5,... | collective-permute-start | bytes 786440 | tf_op jit(solution)/shard_map/ppermute | solution.py:46
  468.5 53.4 %collective-permute-start.88 = (bf16[64,2048]{1,0:T(8,128)(2,1)S(1)}, bf16[64,2048]{1,0:T(8,128)(2,1)}, u32[]{:S(2)}, u32[]{:S(2)}) collective-permute-start(bf16[64,2048]{1,0:T(8,128)(2,1)S(1)} %broadcast_select_fusion.5), channel_id=1, source_target_pairs={{0,16},{1,17},{16,0},{17,1},{2,18},{3,19},{18,2},{19,3},{4,20},{5,... | collective-permute-start | bytes 786440 | tf_op jit(solution)/shard_map/ppermute | solution.py:46
  513.5 38.1 %collective-permute-start.54 = (bf16[128,2048]{1,0:T(8,128)(2,1)S(1)}, bf16[128,2048]{1,0:T(8,128)(2,1)}, u32[]{:S(2)}, u32[]{:S(2)}) collective-permute-start(bf16[128,2048]{1,0:T(8,128)(2,1)S(1)} %fusion.12), channel_id=1, source_target_pairs={{1,8},{8,1},{3,10},{10,3},{5,12},{12,5},{7,14},{14,7},{17,24},{24,... | collective-permute-start | bytes 1572872 | tf_op jit(solution)/shard_map/ppermute | solution.py:23
  517.7 44.1 %collective-permute-start.80 = (bf16[2,4,32,1024]{3,2,1,0:T(8,128)(2,1)S(1)}, bf16[2,4,32,1024]{3,2,1,0:T(8,128)(2,1)}, u32[]{:S(2)}, u32[]{:S(2)}) collective-permute-start(bf16[2,4,32,1024]{3,2,1,0:T(8,128)(2,1)S(1)} %pad_maximum_fusion.1.refs_0_), channel_id=1, source_target_pairs={{0,32},{32,64},{64,96},{96,0},{1,33},{33,65},{65,97},{97,1},{2,34}... | collective-permute-start | bytes 1572872 | tf_op jit(solution)/shard_map/ppermute | solution.py:41
  520.0 69.2 %collective-permute-start.81 = (bf16[2,4,32,1024]{3,2,1,0:T(8,128)(2,1)S(1)}, bf16[2,4,32,1024]{3,2,1,0:T(8,128)(2,1)}, u32[]{:S(2)}, u32[]{:S(2)}) collective-permute-start(bf16[2,4,32,1024]{3,2,1,0:T(8,128)(2,1)S(1)} %pad_maximum_fusion.1.refs_0_), channel_id=1, source_target_pairs={{0,64},{32,96},{64,0},{96,32},{1,65},{33,97},{65,1},{97,33},{2,66}... | collective-permute-start | bytes 1572872 | tf_op jit(solution)/shard_map/ppermute | solution.py:41
  521.1 68.1 %collective-permute-start.82 = (bf16[2,4,32,1024]{3,2,1,0:T(8,128)(2,1)S(1)}, bf16[2,4,32,1024]{3,2,1,0:T(8,128)(2,1)}, u32[]{:S(2)}, u32[]{:S(2)}) collective-permute-start(bf16[2,4,32,1024]{3,2,1,0:T(8,128)(2,1)S(1)} %pad_maximum_fusion.1.refs_0_), channel_id=1, source_target_pairs={{0,96},{32,0},{64,32},{96,64},{1,97},{33,1},{65,33},{97,65},{2,98}... | collective-permute-start | bytes 1572872 | tf_op jit(solution)/shard_map/ppermute | solution.py:41
  523.0 83.4 %all-to-all-start = ((bf16[16,32,2048]{2,1,0:T(8,128)(2,1)}), bf16[16,32,2048]{2,1,0:T(8,128)(2,1)}, u32[]{:S(2)}, u32[]{:S(2)}) async-start(bf16[16,32,2048]{2,1,0:T(8,128)(2,1)} %fusion.2), calls=%async_computation | async-start | bytes 4194304 | tf_op jit(solution)/shard_map/all_to_all | solution.py:617
  617.0 55.2 %collective-permute-start.92 = (bf16[4,2,64,2048]{3,2,1,0:T(8,128)(2,1)}, bf16[4,2,64,2048]{3,2,1,0:T(8,128)(2,1)S(1)}, u32[]{:S(2)}, u32[]{:S(2)}) collective-permute-start(bf16[4,2,64,2048]{3,2,1,0:T(8,128)(2,1)} %bitcast_dynamic-update-slice_fusion), channel_id=1, source_target_pairs={{0,8},{8,0},{1,9},{9,1},{2,10},{10,2},{3,11},{11,3},{4,12},{12,4},... | collective-permute-start | bytes 6291464 | tf_op jit(solution)/shard_map/ppermute | solution.py:33
  (132 other events, 1758.7 us)
Sparse Core Ops, SparseCore 0:
  34.4 42.0 all-gather.3
  78.3 46.9 all-gather.5
  153.6 51.6 all-gather.7
